TPU v7x, 512 devices: a whole 4x8x8 slice. The times are simulated.
512 devices in a mesh: bcast: 32 (over x_lo, z, core), grad: 16 (over x_hi, y).
Axes of the slice: x: 4 (x_hi: 2, x_lo: 2; x = x_hi * 2 + x_lo), y: 8, z: 8, core: 2. Of those that a mesh axis runs over, the one named last changes fastest.
Arguments:
- activations: bfloat16 [32768, 16, 1024], P('bcast', 'grad'), may hold values from -150 to 150
- gradient: bfloat16 [6144, 16, 1024], P(('bcast', 'grad')), may hold values from -6 to 6
- block_map: int32 [16], replicated, may hold values from 0 to 15, each once
Outputs:
- precond: bfloat16 [6144, 16, 1024], P('bcast', 'grad')
Inputs may be any that keep to these rules, and one draw needn't show every extreme that they name: `block_map`: each factor block appears exactly once.
All inputs are finite; a program needn't handle non-finite values.
Results may differ from a plain program's by a relative error of at most 0.0066.
Values may be sent and summed in bfloat16 or wider, within the bound.
A program may use at most 128 MiB of HBM per device.

v0:
```python
import jax
import jax.numpy as jnp
from jax import lax
from jax.sharding import PartitionSpec as P


def spread(block, axis, owner):
    block = jnp.where(lax.axis_index(axis) == owner, block, jnp.zeros_like(block))
    return lax.psum(block, axis)


def inverse_root(covariance):
    identity = jnp.eye(covariance.shape[0], dtype=jnp.float32)
    lower_factor = jnp.linalg.cholesky(covariance)
    return jax.scipy.linalg.solve_triangular(lower_factor, identity, lower=True).astype(
        jnp.bfloat16
    )


def per_device(activations, gradient, block_map):
    width = activations.shape[2]
    bcast_count = lax.axis_size("bcast")
    token_count = activations.shape[0] * bcast_count
    column = lax.axis_index("grad")
    identity = jnp.eye(width, dtype=jnp.float32)
    act_rows = activations[:, 0, :]
    partial_cov = lax.dot_general(
        act_rows, act_rows, (((0,), (0,)), ((), ())), preferred_element_type=jnp.float32
    )
    summed = lax.psum(partial_cov, "bcast")
    covariance = summed / token_count + identity
    owner_index = column % bcast_count
    local_root = lax.cond(
        lax.axis_index("bcast") == owner_index,
        inverse_root,
        lambda values: jnp.zeros((width, width), jnp.bfloat16),
        covariance,
    )
    root_factor = spread(local_root, "bcast", owner_index)
    chooser = (block_map == column).astype(jnp.bfloat16)
    chosen = jnp.einsum(
        "rkb,k->rb",
        lax.all_gather(gradient, "grad", axis=0, tiled=True),
        chooser,
        preferred_element_type=jnp.float32,
    ).astype(jnp.bfloat16)
    half_done = lax.dot_general(
        chosen, root_factor, (((1,), (1,)), ((), ())), preferred_element_type=jnp.float32
    ).astype(jnp.bfloat16)
    result = jnp.dot(half_done, root_factor, preferred_element_type=jnp.float32).astype(
        jnp.bfloat16
    )
    return result[:, None, :]


def solution(mesh):
    return jax.shard_map(
        per_device,
        mesh=mesh,
        in_specs=(P("bcast", "grad", None), P(("bcast", "grad"), None, None), P()),
        out_specs=P("bcast", "grad", None),
        check_vma=False,
    )
```

profile of v0, /device:TPU:1, one launch (start us, length us, event | category | flops | bytes accessed | tf_op | source)
XLA Modules:
  0.0 870.5 jit_solution(2724609655259298417)
XLA Ops:
  7.4 0.0 copy-start
  7.4 0.0 all-reduce.4.cloned.1.call-start
  7.4 1.6 copy-done
  9.0 4.4 fusion.72
  13.3 0.0 all-reduce.4.cloned.1.call-update
  13.3 0.0 all-gather.2.cloned.1.call-start
  13.4 0.5 all-gather.2.cloned.1.call-update
  13.9 0.0 all-reduce.6.cloned.1.call-start
  14.0 2.6 fusion.71
  16.6 245.4 %all-reduce.4.cloned.1.call-done = f32[1024,1024]{1,0:T(8,128)} async-done(((f32[1024,1024]{1,0:T(8,128)}), f32[1024,1024]{1,0:T(8,128)}) %all-reduce.4.cloned.1.call-update) | async-done | bytes 4194320 | tf_op jit(solution)/shard_map/psum | solution.py:30
  261.9 1.6 conditional.1
  261.9 1.6 broadcast.365
  263.5 0.0 copy-start.3
  263.5 1.5 broadcast_select_fusion
  265.0 0.0 all-reduce.6.cloned.1.call-update
  265.0 0.0 all-gather.2.cloned.1.call-done
  265.0 0.0 copy-done.3
  265.1 0.0 copy-start.1
  265.1 4.0 fusion.75
  269.1 589.7 %all-reduce.6.cloned.1.call-done = bf16[1024,1024]{1,0:T(8,128)(2,1)} async-done(((bf16[1024,1024]{1,0:T(8,128)(2,1)}), bf16[1024,1024]{1,0:T(8,128)(2,1)}) %all-reduce.6.cloned.1.call-update) | async-done | bytes 2097168 | tf_op jit(solution)/shard_map/psum | solution.py:9
  858.8 4.3 fusion.74
  863.1 0.0 copy-done.1
Async XLA Ops:
  7.4 1.6 copy-start
  7.4 254.6 %all-reduce.4.cloned.1.call-start = ((), (), s32[]{:S(2)}) async-start(), calls=%async_computation.1 | async-start | bytes 8388608 | tf_op jit(solution)/shard_map/psum | solution.py:30
  13.3 251.7 %all-gather.2.cloned.1.call-start = ((), (), s32[]{:S(2)}) async-start(), calls=%async_computation | async-start | bytes 6684672 | tf_op jit(solution)/shard_map/all_gather | solution.py:43
  13.9 844.9 %all-reduce.6.cloned.1.call-start = ((), (), s32[]{:S(2)}) async-start(), calls=%async_computation.2 | async-start | bytes 4194304 | tf_op jit(solution)/shard_map/psum | solution.py:9
  263.5 1.5 copy-start.3
  265.1 598.1 %copy-start.1 = (bf16[1024,1,1024]{2,0,1:T(8,128)(2,1)S(1)}, bf16[1024,1,1024]{2,0,1:T(8,128)(2,1)}, u32[]{:S(2)}) copy-start(bf16[1024,1,1024]{2,0,1:T(8,128)(2,1)} %param.5) | copy-start | bytes 6291460
Sparse Core Ops, SparseCore 0:
  13.5 248.4 all-reduce.3
  265.1 593.6 all-reduce.5
Sparse Core Ops, SparseCore 1:
  17.5 132.7 all-gather.1
where the time goes:
time: 875 us; the launch traced here: 871 us
  waiting for transfers between devices  836 us (96%)
  between operations  14.9 us (2%)
  matrix products  12.6 us (1%)
    psum x1, waiting for transfers between devices, spread(): return lax.psum(block, axis)  590 us
    psum x1, waiting for transfers between devices, per_device(): summed = lax.psum(partial_cov, 'bcast')  245 us
  transfers between devices with their start and end apart: 3, of which 2 were waited for; matrix products, arithmetic and copies ran while one was open for 1% of the time, Pallas kernels for 0%

commit v1 on v0

v1 whole, which is shorter than its diff:
```python
import functools

import jax
import jax.numpy as jnp
from jax import lax
from jax.experimental import pallas as pl
from jax.experimental.pallas import tpu as pltpu
from jax.sharding import PartitionSpec as P

MESH = pl.DeviceIdType.MESH
F32, BF16 = jnp.float32, jnp.bfloat16
B = 128


def block_rows(i, j):
    return (j * 8 - j * (j - 1) // 2 + (i - j)) * B


def covariance_kernel(act_ref, out_ref):
    for j in range(8):
        column = act_ref[:, j * B : (j + 1) * B]
        part = lax.dot_general(
            act_ref[:, j * B :], column, (((0,), (0,)), ((), ())), preferred_element_type=F32
        )
        out_ref[pl.ds(block_rows(j, j), (8 - j) * B), :] = part


def exchange_kernel(part_ref, grad_ref, sum_ref, tile_ref, acc, from_core, plus, minus, from_x,
                    core_s, core_r, plus_s, plus_r, minus_s, minus_r, x_s, x_r,
                    gx_s, gx_r, gp_s, gp_r, gm_s, gm_r, gc_s, gc_r, grad_s, grad_r, own_sem):
    HALF, CHUNK, SUB = 2304, 288, 144
    me = lax.axis_index("bcast")
    column = lax.axis_index("grad")
    core, z, x = me % 2, (me // 2) % 8, me // 16
    at = lambda c, zz, xx: {"bcast": xx * 16 + (zz % 8) * 2 + c}
    twin, up, down, across = at(1 - core, z, x), at(core, z + 1, x), at(core, z + 7, x), at(core, z, 1 - x)

    barrier = pltpu.get_barrier_semaphore()
    for peer in (twin, up, down, across):
        pl.semaphore_signal(barrier, inc=1, device_id=peer, device_id_type=MESH)
    for d in range(1, 16):
        pl.semaphore_signal(barrier, inc=1, device_id={"grad": (column + d) % 16}, device_id_type=MESH)
    pl.semaphore_wait(barrier, 19)

    def send(src, dst, s, r, to):
        c = pltpu.make_async_remote_copy(src_ref=src, dst_ref=dst, send_sem=s, recv_sem=r,
                                         device_id=to, device_id_type=MESH)
        c.start()
        return c

    def rows(q, h=None):
        if h is None:
            return pl.ds((q % 8) * CHUNK, CHUNK)
        return pl.ds((q % 8) * CHUNK + h * SUB, SUB)

    def half_rows(c, q, h=None):
        if h is None:
            return pl.ds(c * HALF + (q % 8) * CHUNK, CHUNK)
        return pl.ds(c * HALF + (q % 8) * CHUNK + h * SUB, SUB)

    order = [4, 5, 3, 6, 2, 7, 1, 0]
    waits = []
    cores = {}
    for n, d in enumerate(order):
        cores[d] = send(part_ref.at[half_rows(1 - core, z + d)], from_core.at[rows(z + d)],
                        core_s.at[n], core_r.at[n], twin)
    tiles = []
    for d in range(1, 16):
        to = (column + d) % 16
        tiles.append(send(grad_ref.at[to], tile_ref.at[column], grad_s.at[d], grad_r.at[d], {"grad": to}))
    own = pltpu.make_async_copy(grad_ref.at[column], tile_ref.at[column], own_sem)
    own.start()

    for n, d in enumerate(order):
        cores[d].wait_recv()
        acc[rows(z + d)] = part_ref[half_rows(core, z + d)] + from_core[rows(z + d)]
        if d == 4:
            p = [send(acc.at[rows(z + 4, h)], plus.at[0, h], plus_s.at[0, h], plus_r.at[0, h], up) for h in (0, 1)]
            waits += p
        if d == 5:
            m = [send(acc.at[rows(z + 5, h)], minus.at[0, h], minus_s.at[0, h], minus_r.at[0, h], down) for h in (0, 1)]
            waits += m
    for s in range(1, 4):
        q = []
        for h in (0, 1):
            p[h].wait_recv()
            acc[rows(z + 4 - s, h)] += plus[s - 1, h]
            q.append(send(acc.at[rows(z + 4 - s, h)], plus.at[s, h], plus_s.at[s, h], plus_r.at[s, h], up))
        p = q
        waits += q
        if s < 3:
            q = []
            for h in (0, 1):
                m[h].wait_recv()
                acc[rows(z + 5 + s, h)] += minus[s - 1, h]
                q.append(send(acc.at[rows(z + 5 + s, h)], minus.at[s, h], minus_s.at[s, h], minus_r.at[s, h], down))
            m = q
            waits += q
    for h in (0, 1):
        m[h].wait_recv()
        acc[rows(z, h)] += minus[2, h]
    for h in (0, 1):
        p[h].wait_recv()
        acc[rows(z, h)] += plus[3, h]
    cx = send(acc.at[rows(z, 1 - x)], from_x, x_s, x_r, across)
    cx.wait_recv()
    mine = half_rows(core, z, x)
    sum_ref[mine] = acc[rows(z, x)] + from_x[...]
    waits.append(cx)
    gx = send(sum_ref.at[mine], sum_ref.at[mine], gx_s, gx_r, across)
    waits.append(gx)
    def chunk_send(q, h, sem_s, sem_r, k, hh, to):
        r = half_rows(core, q, h)
        return send(sum_ref.at[r], sum_ref.at[r], sem_s.at[k, hh], sem_r.at[k, hh], to)
    P0, M0 = [None, None], [None, None]
    for k, h in ((0, x), (1, 1 - x)):
        if k == 1:
            gx.wait_recv()
        P0[k] = chunk_send(z, h, gp_s, gp_r, 0, k, up)
        M0[k] = chunk_send(z, h, gm_s, gm_r, 0, k, down)
    waits += P0 + M0
    fin = []
    r = half_rows(core, z)
    fin.append(send(sum_ref.at[r], sum_ref.at[r], gc_s.at[0], gc_r.at[0], twin))
    for s in range(1, 5):
        Q = []
        for k, h in ((0, x), (1, 1 - x)):
            P0[k].wait_recv()
            if s < 4:
                Q.append(chunk_send(z - s + 8, h, gp_s, gp_r, s, k, up))
        P0 = Q
        waits += Q
        r = half_rows(core, z - s + 8)
        fin.append(send(sum_ref.at[r], sum_ref.at[r], gc_s.at[s], gc_r.at[s], twin))
        if s < 4:
            Q = []
            for k, h in ((0, x), (1, 1 - x)):
                M0[k].wait_recv()
                if s < 3:
                    Q.append(chunk_send(z + s, h, gm_s, gm_r, s, k, down))
            M0 = Q
            waits += Q
            r = half_rows(core, z + s)
            fin.append(send(sum_ref.at[r], sum_ref.at[r], gc_s.at[4 + s], gc_r.at[4 + s], twin))
    for c in fin:
        c.wait()
    for c in waits:
        c.wait_send()
    for d in range(8):
        cores[order[d]].wait_send()
    for c in tiles:
        c.wait()
    own.wait()


def exchange(part, grads):
    dma = pltpu.SemaphoreType.DMA
    vm = pl.BlockSpec(memory_space=pltpu.VMEM)
    return pl.pallas_call(
        exchange_kernel,
        out_shape=(jax.ShapeDtypeStruct((4608, B), F32), jax.ShapeDtypeStruct(grads.shape, BF16)),
        in_specs=[vm, vm],
        out_specs=(vm, vm),
        scratch_shapes=[
            pltpu.VMEM((2304, B), F32), pltpu.VMEM((2304, B), F32),
            pltpu.VMEM((4, 2, 144, B), F32), pltpu.VMEM((3, 2, 144, B), F32), pltpu.VMEM((144, B), F32),
            dma((8,)), dma((8,)), dma((4, 2)), dma((4, 2)), dma((3, 2)), dma((3, 2)), dma, dma,
            dma, dma, dma((4, 2)), dma((4, 2)), dma((3, 2)), dma((3, 2)), dma((8,)), dma((8,)),
            dma((16,)), dma((16,)), dma,
        ],
        compiler_params=pltpu.CompilerParams(collective_id=0, has_side_effects=True, vmem_limit_bytes=48 << 20),
    )(part, grads)


def covariance(act):
    vm = pl.BlockSpec(memory_space=pltpu.VMEM)
    return pl.pallas_call(
        covariance_kernel,
        out_shape=jax.ShapeDtypeStruct((4608, B), F32),
        in_specs=[vm], out_specs=vm,
        compiler_params=pltpu.CompilerParams(vmem_limit_bytes=48 << 20),
    )(act)


def lb(t,j): return jnp.broadcast_to(t[:,j:j+1],(8,128))
def sb(t,r): return jnp.broadcast_to(t[r:r+1,:],(8,128))
def tsum(xs):
    xs=list(xs)
    while len(xs)>1:
        xs=[xs[i]+xs[i+1] if i+1<len(xs) else xs[i] for i in range(0,len(xs),2)]
    return xs[0]
def split(x):
    h=x.astype(BF16); r=x-h.astype(F32); m=r.astype(BF16); l=(r-m.astype(F32)).astype(BF16)
    return h,m,l
def gj(L,R,p,sub,two):
    nv=p//8
    if not two:
        for j in range(p):
            u,r=j//8,j%8
            dinv=1.0/sb(L[u][j],r)
            isr=sub==r
            t=sb(R[u],r)*dinv
            for k in range(j+1,p):
                tk=sb(L[u][k],r)*dinv
                for a in range(nv):
                    y=L[a][k]-L[a][j]*tk
                    L[a][k]=jnp.where(isr,tk,y) if a==u else y
            R=[R[a]-L[a][j]*t for a in range(nv)]
            R[u]=jnp.where(isr,t,R[u])
        return R
    for j in range(0,p,2):
        u,r=j//8,j%8
        a_=sb(L[u][j],r); b_=sb(L[u][j+1],r); c_=sb(L[u][j+1],r+1)
        idet=1.0/(a_*c_-b_*b_)
        p00=c_*idet; p11=a_*idet; p01=b_*idet
        is0=sub==r; is1=sub==r+1
        def upd(cols):
            s0=sb(cols[u],r); s1=sb(cols[u],r+1)
            t0=p00*s0-p01*s1; t1=p11*s1-p01*s0
            out=[cols[a]-(L[a][j]*t0+L[a][j+1]*t1) for a in range(nv)]
            out[u]=jnp.where(is0,t0,jnp.where(is1,t1,out[u]))
            return out
        for k in range(j+2,p):
            o=upd([L[a][k] for a in range(nv)])
            for a in range(nv): L[a][k]=o[a]
        R=upd(R)
    return R
def inv128_ref(X_ref,two=False,p=16):
    lane=lax.broadcasted_iota(jnp.int32,(8,128),1)
    sub=lax.broadcasted_iota(jnp.int32,(8,128),0)
    lane_all=lax.broadcasted_iota(jnp.int32,(128,128),1)
    nv=p//8
    G=128//p
    R=[X_ref[8*a:8*a+8,:] for a in range(nv)]
    for g in range(G):
        base=g*p; n=(g+1)%G
        N=[X_ref[n*p+8*a:n*p+8*a+8,:] for a in range(nv)]
        ing=(lane>=base)&(lane<base+p)
        L=[[lb(R[a],base+j) for j in range(p)] for a in range(nv)]
        Rh=[jnp.where(ing,jnp.where(lane-base==sub+8*a,1.0,0.0),R[a]) for a in range(nv)]
        X=X_ref[...]
        h,m,l=split(X)
        LH=jnp.concatenate([h,h,m,h,l,m],axis=1)
        if g<G-1:
            CN=[[lb(N[a],base+j) for j in range(p)] for a in range(nv)]
        T=gj(L,Rh,p,sub,two)
        Tc=jnp.concatenate(T,axis=0)
        if g<G-1:
            Ts=[sb(T[j//8],j%8) for j in range(p)]
            Nn=[jnp.where(ing,0.0,N[a])-tsum([CN[a][j]*Ts[j] for j in range(p)]) for a in range(nv)]
        th,tm,tl=split(Tc)
        def pad(t):
            parts=[]
            if base: parts.append(jnp.zeros((base,128),BF16))
            parts.append(t)
            if base+p<128: parts.append(jnp.zeros((128-base-p,128),BF16))
            return jnp.concatenate(parts,axis=0)
        th,tm,tl=pad(th),pad(tm),pad(tl)
        RH=jnp.concatenate([th,tm,th,tl,th,tm],axis=0)
        U=jnp.dot(LH,RH,preferred_element_type=F32)
        inga=(lane_all>=base)&(lane_all<base+p)
        Xn=jnp.where(inga,0.0,X)-U
        X_ref[...]=Xn
        X_ref[base:base+p,:]=Tc
        if g<G-1:
            for a in range(nv): X_ref[n*p+8*a:n*p+8*a+8,:]=Nn[a]
            R=Nn


def lform(x):
    h,m,l=split(x); return jnp.concatenate([h,h,m,h,l,m],axis=1)
def rform(x):
    h,m,l=split(x); return jnp.concatenate([h,m,h,l,h,m],axis=1)
NT=(((1,),(1,)),((),()))
def nt(a,b): return lax.dot_general(a,b,NT,preferred_element_type=F32)
def factor_kernel(unroll,KA,KG,tokens,s_ref,g_ref,o_ref,A,X,G,Mh,Mm,Yh,Ym,MG):
    eye=jnp.where(lax.broadcasted_iota(jnp.int32,(B,B),0)==lax.broadcasted_iota(jnp.int32,(B,B),1),1.0,0.0).astype(F32)
    scale=1.0/tokens
    for j in range(8):
        for i in range(j,8):
            r=block_rows(i,j)
            v=s_ref[r:r+B,:]*scale
            A[r:r+B,:]=v+eye if i==j else v
    G[...]=g_ref[...].astype(F32)
    def body(j):
        R=(7-j)*B; d=block_rows(j,j); c=d+B
        dcat=rform(X[...])
        gl=lform(G[:,j*B:(j+1)*B])
        mg=nt(gl[:,:KG],dcat[:,:KG])
        MG[:,j*B:(j+1)*B]=mg
        if R:
            col=A[c:c+R,:]
            ccat=lform(col)
            m=nt(ccat[:,:KA],dcat[:,:KA])
            mcat=rform(m)
            Mh[c:c+R,:]=mcat[:,0:B]; Mm[c:c+R,:]=mcat[:,B:2*B]
            for k in range(j+1,8):
                o=(k-j-1)*B
                rk=block_rows(k,k); n=(8-k)*B
                A[rk:rk+n,:]-=nt(mcat[o:R,:KA],ccat[o:o+B,:KA])
            gm=rform(mg)
            G[:,(j+1)*B:]-=nt(gm[:,:KG],ccat[:,:KG])
    if unroll:
        for j in range(8):
            d=block_rows(j,j)
            X[...]=A[d:d+B,:]
            inv128_ref(X)
            body(j)
    else:
        def it(j,carry):
            d=pl.multiple_of((j*8-j*(j-1)//2)*B,B)
            X[...]=A[pl.ds(d,B),:]
            inv128_ref(X)
            for jj in range(8):
                @pl.when(j==jj)
                def _(): body(jj)
            return carry
        lax.fori_loop(0,8,it,0)
    for j in range(7,-1,-1):
        y=MG[:,j*B:(j+1)*B]
        if j<7:
            c=block_rows(j,j)+B; R=(7-j)*B
            yh,ym=Yh[:,(j+1)*B:],Ym[:,(j+1)*B:]
            mh,mm=Mh[c:c+R,:],Mm[c:c+R,:]
            y=y-(jnp.dot(yh,mh,preferred_element_type=F32)+jnp.dot(yh,mm,preferred_element_type=F32)+jnp.dot(ym,mh,preferred_element_type=F32))
        h=y.astype(BF16)
        Yh[:,j*B:(j+1)*B]=h
        Ym[:,j*B:(j+1)*B]=(y-h.astype(F32)).astype(BF16)
        o_ref[:,j*B:(j+1)*B]=h
def factor(s,g,tokens,unroll=False,KA=384,KG=384):
    vm=pl.BlockSpec(memory_space=pltpu.VMEM)
    n=g.shape[0]
    return pl.pallas_call(functools.partial(factor_kernel,unroll,KA,KG,tokens),
      out_shape=jax.ShapeDtypeStruct((n,1024),BF16),in_specs=[vm,vm],out_specs=vm,
      scratch_shapes=[pltpu.VMEM((4608,B),F32),pltpu.VMEM((B,B),F32),pltpu.VMEM((n,1024),F32),pltpu.VMEM((4608,B),BF16),pltpu.VMEM((4608,B),BF16),
        pltpu.VMEM((n,1024),BF16),pltpu.VMEM((n,1024),BF16),pltpu.VMEM((n,1024),F32)],
      compiler_params=pltpu.CompilerParams(vmem_limit_bytes=56<<20))(s,g)


def per_device(activations, gradient, block_map):
    tokens = activations.shape[0] * lax.axis_size("bcast")
    rows = gradient.shape[0]
    part = covariance(activations[:, 0, :])
    chooser = (block_map[None, :] == jnp.arange(16, dtype=jnp.int32)[:, None]).astype(BF16)
    ordered = jnp.einsum("kj,rjb->krb", chooser, gradient, preferred_element_type=F32).astype(BF16)
    total, tiles = exchange(part, ordered.reshape(16, rows * 8, 128))
    return factor(total, tiles.reshape(16 * rows, 1024), tokens)[:, None, :]


def solution(mesh):
    return jax.shard_map(
        per_device,
        mesh=mesh,
        in_specs=(P("bcast", "grad", None), P(("bcast", "grad"), None, None), P()),
        out_specs=P("bcast", "grad", None),
        check_vma=False,
    )
```

time: 875 us -> 99.7 us (0.11)
  waiting for transfers between devices: 836 us -> 0 us
  Pallas kernels: 0 us -> 94.7 us
  between operations: 14.9 us -> 0.05 us
  matrix products: 12.6 us -> 0.9 us
    psum x2 -> x0, waiting for transfers between devices: 835 us -> none  [the longest x1 590 us: spread(): return lax.psum(block, axis)]
    pallas_call x0 -> x3, Pallas kernels: none -> 94.7 us  [the longest x1 57.9 us: exchange(): pl.pallas_call(exchange_kernel, out_shape=(jax.ShapeDtypeStruct((4608, B)...]
    dot_general x3 -> x1, matrix products: 12.6 us -> 0.9 us  [per_device(): jnp.einsum('kj,rjb->krb', chooser, gradient, preferred_element_type=F32)]
  transfers between devices with their start and end apart: 3 -> 0, of which waited for: 2 -> 0; matrix products, arithmetic and copies ran while one was open for 1% -> 0% of each run, Pallas kernels for 0% -> 0%
where the time goes in v1:
time: 99.7 us; the launch traced here: 99.5 us
  Pallas kernels  94.7 us (95%)
  local copies, waits for them, and re-layouts  3.83 us (4%)
    pallas_call x1, Pallas kernels, exchange(): pl.pallas_call(exchange_kernel, out_shape=(jax.ShapeDtypeStruct((4608, B)...  57.9 us
    pallas_call x1, Pallas kernels, factor(): pl.pallas_call(functools.partial(factor_kernel, unroll, KA, KG, tokens),...  34.2 us
    pallas_call x1, Pallas kernels, covariance(): pl.pallas_call(covariance_kernel, out_shape=jax.ShapeDtypeStruct((4608, B...  2.69 us
    unnamed x6, local copies, waits for them, and re-layouts  2.41 us

profile of v1, /device:TPU:1, one launch (start us, length us, event | category | flops | bytes accessed | tf_op | source)
XLA Modules:
  0.0 99.5 jit_solution(12029276002991788552)
XLA Ops:
  0.0 0.0 copy-start
  0.0 0.0 copy-start.2
  0.0 1.0 copy-done
  1.0 0.9 convolution_convert_fusion
  1.9 0.2 copy.5
  2.1 0.3 reshape.7.grad_ref
  2.4 0.0 copy-done.2
  2.4 2.7 %shard_map.37.part_ref = f32[4608,128]{1,0:T(8,128)S(1)} custom-call(bf16[1024,1024]{1,0:T(8,128)(2,1)S(1)} %bitcast.6), custom_call_target="tpu_custom_call" | custom-call | tf_op jit(solution)/shard_map/pallas_call | solution.py:177
  5.1 57.9 %shard_map.38 = (f32[4608,128]{1,0:T(8,128)S(1)}, bf16[16,96,128]{2,1,0:T(8,128)(2,1)S(1)}) custom-call(f32[4608,128]{1,0:T(8,128)S(1)} %shard_map.37.part_ref, bf16[16,96,128]{2,1,0:T(8,128)(2,1)S(1)} %reshape.7.grad_ref), custom_call_target="tpu_custom_call" | custom-call | tf_op jit(solution)/shard_map/pallas_call | solution.py:159
  63.0 0.0 copy-start.1
  63.0 1.4 %copy-done.1 = f32[4608,128]{1,0:T(8,128)} copy-done((f32[4608,128]{1,0:T(8,128)}, f32[4608,128]{1,0:T(8,128)S(1)}, u32[]{:S(2)}) %copy-start.1) | copy-done | bytes 2359320
  64.4 0.9 reshape.8.g_ref
  65.3 34.2 %shard_map.39 = bf16[192,1024]{1,0:T(8,128)(2,1)} custom-call(f32[4608,128]{1,0:T(8,128)} %copy-done.1, bf16[192,1024]{1,0:T(8,128)(2,1)} %reshape.8.g_ref), custom_call_target="tpu_custom_call" | custom-call | tf_op jit(solution)/shard_map/pallas_call | solution.py:333
Async XLA Ops:
  0.0 1.0 %copy-start = (bf16[12,16,1024]{2,1,0:T(8,128)(2,1)S(1)}, bf16[12,16,1024]{2,1,0:T(8,128)(2,1)}, u32[]{:S(2)}) copy-start(bf16[12,16,1024]{2,1,0:T(8,128)(2,1)} %param.4) | copy-start | bytes 1179652
  0.0 2.4 %copy-start.2 = (bf16[1024,1,1024]{2,0,1:T(8,128)(2,1)S(1)}, bf16[1024,1,1024]{2,0,1:T(8,128)(2,1)}, u32[]{:S(2)}) copy-start(bf16[1024,1,1024]{2,0,1:T(8,128)(2,1)} %param.3) | copy-start | bytes 6291460
  63.0 1.4 %copy-start.1 = (f32[4608,128]{1,0:T(8,128)}, f32[4608,128]{1,0:T(8,128)S(1)}, u32[]{:S(2)}) copy-start(f32[4608,128]{1,0:T(8,128)S(1)} %get-tuple-element.7.s_ref) | copy-start | bytes 7077892

commit v2 on v1

--- a/solution.py
+++ b/solution.py
@@ -25,16 +25,19 @@
         out_ref[pl.ds(block_rows(j, j), (8 - j) * B), :] = part
 
 
-def exchange_kernel(part_ref, grad_ref, sum_ref, tile_ref, acc, from_core, plus, minus, from_x,
-                    core_s, core_r, plus_s, plus_r, minus_s, minus_r, x_s, x_r,
-                    gx_s, gx_r, gp_s, gp_r, gm_s, gm_r, gc_s, gc_r, grad_s, grad_r, own_sem):
-    HALF, CHUNK, SUB = 2304, 288, 144
+def exchange_body(part_ref, grad_ref, sum_ref, tile_ref, acc, from_core, from_x, za_plus, za_minus, zb_plus, zb_minus, xa,
+                  s_sem, r_sem, own_sem):
+    H = 1152
+    CA, SA = 144, 72
+    XB, CB = 576, 72
     me = lax.axis_index("bcast")
     column = lax.axis_index("grad")
     core, z, x = me % 2, (me // 2) % 8, me // 16
-    at = lambda c, zz, xx: {"bcast": xx * 16 + (zz % 8) * 2 + c}
+
+    def at(c, zz, xx):
+        return {"bcast": xx * 16 + (zz % 8) * 2 + c}
+
     twin, up, down, across = at(1 - core, z, x), at(core, z + 1, x), at(core, z + 7, x), at(core, z, 1 - x)
-
     barrier = pltpu.get_barrier_semaphore()
     for peer in (twin, up, down, across):
         pl.semaphore_signal(barrier, inc=1, device_id=peer, device_id_type=MESH)
@@ -42,131 +45,200 @@
         pl.semaphore_signal(barrier, inc=1, device_id={"grad": (column + d) % 16}, device_id_type=MESH)
     pl.semaphore_wait(barrier, 19)
 
-    def send(src, dst, s, r, to):
-        c = pltpu.make_async_remote_copy(src_ref=src, dst_ref=dst, send_sem=s, recv_sem=r,
+    sent = []
+
+    def send(src, dst, to):
+        n = len(sent)
+        c = pltpu.make_async_remote_copy(src_ref=src, dst_ref=dst, send_sem=s_sem.at[n], recv_sem=r_sem.at[n],
                                          device_id=to, device_id_type=MESH)
         c.start()
+        sent.append(c)
         return c
 
-    def rows(q, h=None):
-        if h is None:
-            return pl.ds((q % 8) * CHUNK, CHUNK)
-        return pl.ds((q % 8) * CHUNK + h * SUB, SUB)
-
-    def half_rows(c, q, h=None):
-        if h is None:
-            return pl.ds(c * HALF + (q % 8) * CHUNK, CHUNK)
-        return pl.ds(c * HALF + (q % 8) * CHUNK + h * SUB, SUB)
+    def ds(start, n):
+        return pl.ds(pl.multiple_of(start, 8), n)
+
+    def a_rows(q, h=None):
+        return ds((q % 8) * CA + (0 if h is None else h * SA), CA if h is None else SA)
+
+    def b_rows(xx, q=None):
+        return ds(H + xx * XB + (0 if q is None else (q % 8) * CB), XB if q is None else CB)
+
+    def pa(c, q, h=None):
+        return ds(c * H + (q % 8) * CA + (0 if h is None else h * SA), CA if h is None else SA)
+
+    def pb(c, xx, q=None):
+        return ds(2 * H + c * H + xx * XB + (0 if q is None else (q % 8) * CB), XB if q is None else CB)
 
     order = [4, 5, 3, 6, 2, 7, 1, 0]
-    waits = []
-    cores = {}
-    for n, d in enumerate(order):
-        cores[d] = send(part_ref.at[half_rows(1 - core, z + d)], from_core.at[rows(z + d)],
-                        core_s.at[n], core_r.at[n], twin)
+    swap_a = {}
+
+    def swap(d):
+        swap_a[d] = send(part_ref.at[pa(1 - core, z + d)], from_core.at[a_rows(z + d)], twin)
+
+    swap(4), swap(5)
+    swap_b0 = send(part_ref.at[pb(1 - core, 1 - x)], from_core.at[b_rows(1 - x)], twin)
+    for d in order[2:]:
+        swap(d)
+    swap_b1 = send(part_ref.at[pb(1 - core, x)], from_core.at[b_rows(x)], twin)
+
+    def add_a(d):
+        swap_a[d].wait_recv()
+        acc[a_rows(z + d)] = part_ref[pa(core, z + d)] + from_core[a_rows(z + d)]
+
+    def ring(buf, k, rows, to):
+        return send(acc.at[rows], buf.at[k], to)
+
+    add_a(4)
+    ap = [send(acc.at[a_rows(z + 4, h)], za_plus.at[0, h], up) for h in (0, 1)]
+    add_a(5)
+    am = [send(acc.at[a_rows(z + 5, h)], za_minus.at[0, h], down) for h in (0, 1)]
+    swap_b0.wait_recv()
+    acc[b_rows(1 - x)] = part_ref[pb(core, 1 - x)] + from_core[b_rows(1 - x)]
+    bx = {d: send(acc.at[b_rows(1 - x, z + d)], from_x.at[ds(((z + d) % 8) * CB, CB)], across) for d in order}
+    own = pltpu.make_async_copy(grad_ref.at[column], tile_ref.at[column], own_sem)
+    own.start()
     tiles = []
     for d in range(1, 16):
         to = (column + d) % 16
-        tiles.append(send(grad_ref.at[to], tile_ref.at[column], grad_s.at[d], grad_r.at[d], {"grad": to}))
-    own = pltpu.make_async_copy(grad_ref.at[column], tile_ref.at[column], own_sem)
-    own.start()
-
-    for n, d in enumerate(order):
-        cores[d].wait_recv()
-        acc[rows(z + d)] = part_ref[half_rows(core, z + d)] + from_core[rows(z + d)]
-        if d == 4:
-            p = [send(acc.at[rows(z + 4, h)], plus.at[0, h], plus_s.at[0, h], plus_r.at[0, h], up) for h in (0, 1)]
-            waits += p
-        if d == 5:
-            m = [send(acc.at[rows(z + 5, h)], minus.at[0, h], minus_s.at[0, h], minus_r.at[0, h], down) for h in (0, 1)]
-            waits += m
-    for s in range(1, 4):
+        tiles.append(send(grad_ref.at[to], tile_ref.at[column], {"grad": to}))
+    for d in order[2:]:
+        add_a(d)
+    swap_b1.wait_recv()
+    acc[b_rows(x)] = part_ref[pb(core, x)] + from_core[b_rows(x)]
+
+    def step_a(s):
+        nonlocal ap, am
         q = []
         for h in (0, 1):
-            p[h].wait_recv()
-            acc[rows(z + 4 - s, h)] += plus[s - 1, h]
-            q.append(send(acc.at[rows(z + 4 - s, h)], plus.at[s, h], plus_s.at[s, h], plus_r.at[s, h], up))
-        p = q
-        waits += q
-        if s < 3:
+            ap[h].wait_recv()
+            acc[a_rows(z + 4 - s, h)] += za_plus[s - 1, h]
+            if s < 4:
+                q.append(send(acc.at[a_rows(z + 4 - s, h)], za_plus.at[s, h], up))
+        ap = q
+        if s < 4:
             q = []
             for h in (0, 1):
-                m[h].wait_recv()
-                acc[rows(z + 5 + s, h)] += minus[s - 1, h]
-                q.append(send(acc.at[rows(z + 5 + s, h)], minus.at[s, h], minus_s.at[s, h], minus_r.at[s, h], down))
-            m = q
-            waits += q
-    for h in (0, 1):
-        m[h].wait_recv()
-        acc[rows(z, h)] += minus[2, h]
-    for h in (0, 1):
-        p[h].wait_recv()
-        acc[rows(z, h)] += plus[3, h]
-    cx = send(acc.at[rows(z, 1 - x)], from_x, x_s, x_r, across)
-    cx.wait_recv()
-    mine = half_rows(core, z, x)
-    sum_ref[mine] = acc[rows(z, x)] + from_x[...]
-    waits.append(cx)
-    gx = send(sum_ref.at[mine], sum_ref.at[mine], gx_s, gx_r, across)
-    waits.append(gx)
-    def chunk_send(q, h, sem_s, sem_r, k, hh, to):
-        r = half_rows(core, q, h)
-        return send(sum_ref.at[r], sum_ref.at[r], sem_s.at[k, hh], sem_r.at[k, hh], to)
-    P0, M0 = [None, None], [None, None]
-    for k, h in ((0, x), (1, 1 - x)):
-        if k == 1:
-            gx.wait_recv()
-        P0[k] = chunk_send(z, h, gp_s, gp_r, 0, k, up)
-        M0[k] = chunk_send(z, h, gm_s, gm_r, 0, k, down)
-    waits += P0 + M0
-    fin = []
-    r = half_rows(core, z)
-    fin.append(send(sum_ref.at[r], sum_ref.at[r], gc_s.at[0], gc_r.at[0], twin))
+                am[h].wait_recv()
+                acc[a_rows(z + 5 + s, h)] += za_minus[s - 1, h]
+                if s < 3:
+                    q.append(send(acc.at[a_rows(z + 5 + s, h)], za_minus.at[s, h], down))
+            am = q
+
+    def take_x(d):
+        bx[d].wait_recv()
+        acc[b_rows(x, z + d)] += from_x[ds(((z + d) % 8) * CB, CB)]
+
+    bp = bm = None
+
+    def step_b(s):
+        nonlocal bp, bm
+        if s < 4:
+            take_x(4 - s)
+        if s == 4:
+            acc[b_rows(x, z)] += zb_plus_wait()
+        else:
+            if s:
+                bp.wait_recv()
+                acc[b_rows(x, z + 4 - s)] += zb_plus[s - 1]
+            bp = send(acc.at[b_rows(x, z + 4 - s)], zb_plus.at[s], up)
+        if s < 4:
+            take_x((5 + s) % 8)
+            if s:
+                bm.wait_recv()
+                acc[b_rows(x, z + 5 + s)] += zb_minus[s - 1]
+            if s < 3:
+                bm = send(acc.at[b_rows(x, z + 5 + s)], zb_minus.at[s], down)
+
+    def zb_plus_wait():
+        bp.wait_recv()
+        return zb_plus[3]
+
+    step_a(1)
+    step_b(0)
+    step_a(2)
+    step_b(1)
+    step_a(3)
+    step_b(2)
+    step_a(4)
+    xa_c = send(acc.at[a_rows(z, 1 - x)], xa, across)
+    step_b(3)
+    xa_c.wait_recv()
+    sum_ref[pa(core, z, x)] = acc[a_rows(z, x)] + xa[...]
+
+    def same(rows, to):
+        return send(sum_ref.at[rows], sum_ref.at[rows], to)
+
+    xg = same(pa(core, z, x), across)
+    step_b(4)
+    sum_ref[pb(core, x, z)] = acc[b_rows(x, z)]
+    twins, xs = [], []
+
+    def b_out(q, plus, minus):
+        r = pb(core, x, q)
+        p = same(r, up) if plus else None
+        m = same(r, down) if minus else None
+        xs.append((same(r, across), q))
+        twins.append(same(r, twin))
+        return p, m
+
+    bp, bm = b_out(z, True, True)
+    xg.wait_recv()
+    r = pa(core, z)
+    ap, am = same(r, up), same(r, down)
+    twins.append(same(r, twin))
+
+    def relay():
+        c, q = xs.pop(0)
+        c.wait_recv()
+        twins.append(same(pb(core, 1 - x, q), twin))
+
     for s in range(1, 5):
-        Q = []
-        for k, h in ((0, x), (1, 1 - x)):
-            P0[k].wait_recv()
-            if s < 4:
-                Q.append(chunk_send(z - s + 8, h, gp_s, gp_r, s, k, up))
-        P0 = Q
-        waits += Q
-        r = half_rows(core, z - s + 8)
-        fin.append(send(sum_ref.at[r], sum_ref.at[r], gc_s.at[s], gc_r.at[s], twin))
-        if s < 4:
-            Q = []
-            for k, h in ((0, x), (1, 1 - x)):
-                M0[k].wait_recv()
-                if s < 3:
-                    Q.append(chunk_send(z + s, h, gm_s, gm_r, s, k, down))
-            M0 = Q
-            waits += Q
-            r = half_rows(core, z + s)
-            fin.append(send(sum_ref.at[r], sum_ref.at[r], gc_s.at[4 + s], gc_r.at[4 + s], twin))
-    for c in fin:
-        c.wait()
-    for c in waits:
+        bp.wait_recv()
+        bp, _ = b_out(z + 8 - s, s < 4, False)
+        if s < 4:
+            bm.wait_recv()
+            _, bm = b_out(z + s, False, s < 3)
+        ap.wait_recv()
+        r = pa(core, z + 8 - s)
+        if s < 4:
+            ap = same(r, up)
+        twins.append(same(r, twin))
+        if s < 4:
+            am.wait_recv()
+            r = pa(core, z + s)
+            if s < 3:
+                am = same(r, down)
+            twins.append(same(r, twin))
+        relay()
+        if s > 1:
+            relay()
+    relay()
+    for c in twins:
+        c.wait_recv()
+    for c in tiles:
+        c.wait_recv()
+    for c in sent:
         c.wait_send()
-    for d in range(8):
-        cores[order[d]].wait_send()
-    for c in tiles:
-        c.wait()
     own.wait()
+
+
+N_COPIES = 160
 
 
 def exchange(part, grads):
     dma = pltpu.SemaphoreType.DMA
     vm = pl.BlockSpec(memory_space=pltpu.VMEM)
     return pl.pallas_call(
-        exchange_kernel,
+        exchange_body,
         out_shape=(jax.ShapeDtypeStruct((4608, B), F32), jax.ShapeDtypeStruct(grads.shape, BF16)),
         in_specs=[vm, vm],
         out_specs=(vm, vm),
         scratch_shapes=[
-            pltpu.VMEM((2304, B), F32), pltpu.VMEM((2304, B), F32),
-            pltpu.VMEM((4, 2, 144, B), F32), pltpu.VMEM((3, 2, 144, B), F32), pltpu.VMEM((144, B), F32),
-            dma((8,)), dma((8,)), dma((4, 2)), dma((4, 2)), dma((3, 2)), dma((3, 2)), dma, dma,
-            dma, dma, dma((4, 2)), dma((4, 2)), dma((3, 2)), dma((3, 2)), dma((8,)), dma((8,)),
-            dma((16,)), dma((16,)), dma,
+            pltpu.VMEM((2304, B), F32), pltpu.VMEM((2304, B), F32), pltpu.VMEM((576, B), F32),
+            pltpu.VMEM((4, 2, 72, B), F32), pltpu.VMEM((3, 2, 72, B), F32),
+            pltpu.VMEM((4, 72, B), F32), pltpu.VMEM((3, 72, B), F32), pltpu.VMEM((72, B), F32),
+            dma((N_COPIES,)), dma((N_COPIES,)), dma,
         ],
         compiler_params=pltpu.CompilerParams(collective_id=0, has_side_effects=True, vmem_limit_bytes=48 << 20),
     )(part, grads)
@@ -240,7 +312,7 @@
         Rh=[jnp.where(ing,jnp.where(lane-base==sub+8*a,1.0,0.0),R[a]) for a in range(nv)]
         X=X_ref[...]
         h,m,l=split(X)
-        LH=jnp.concatenate([h,h,m,h,l,m],axis=1)
+        LH=jnp.concatenate([h,h,m],axis=1)
         if g<G-1:
             CN=[[lb(N[a],base+j) for j in range(p)] for a in range(nv)]
         T=gj(L,Rh,p,sub,two)
@@ -256,7 +328,7 @@
             if base+p<128: parts.append(jnp.zeros((128-base-p,128),BF16))
             return jnp.concatenate(parts,axis=0)
         th,tm,tl=pad(th),pad(tm),pad(tl)
-        RH=jnp.concatenate([th,tm,th,tl,th,tm],axis=0)
+        RH=jnp.concatenate([th,tm,th],axis=0)
         U=jnp.dot(LH,RH,preferred_element_type=F32)
         inga=(lane_all>=base)&(lane_all<base+p)
         Xn=jnp.where(inga,0.0,X)-U

time: 99.7 us -> 99.5 us (level)
    pallas_call x1, Pallas kernels: 34.2 us -> 33.2 us  [factor(): pl.pallas_call(functools.partial(factor_kernel, unroll, KA, KG, tokens),...]
where the time goes in v2:
time: 99.5 us; the launch traced here: 99.3 us
  Pallas kernels  94.5 us (95%)
  local copies, waits for them, and re-layouts  3.83 us (4%)
    pallas_call x1, Pallas kernels, exchange(): pl.pallas_call(exchange_body, out_shape=(jax.ShapeDtypeStruct((4608, B),...  58.6 us
    pallas_call x1, Pallas kernels, factor(): pl.pallas_call(functools.partial(factor_kernel, unroll, KA, KG, tokens),...  33.2 us
    pallas_call x1, Pallas kernels, covariance(): pl.pallas_call(covariance_kernel, out_shape=jax.ShapeDtypeStruct((4608, B...  2.69 us
    unnamed x6, local copies, waits for them, and re-layouts  2.41 us

profile of v2, /device:TPU:1, one launch (start us, length us, event | category | flops | bytes accessed | tf_op | source)
XLA Modules:
  0.0 99.3 jit_solution(5757314295328019)
XLA Ops:
  0.0 0.0 copy-start
  0.0 0.0 copy-start.2
  0.0 1.0 copy-done
  1.0 0.9 convolution_convert_fusion
  1.9 0.2 copy.5
  2.1 0.3 reshape.7.grad_ref
  2.4 0.0 copy-done.2
  2.4 2.7 %shard_map.37.part_ref = f32[4608,128]{1,0:T(8,128)S(1)} custom-call(bf16[1024,1024]{1,0:T(8,128)(2,1)S(1)} %bitcast.6), custom_call_target="tpu_custom_call" | custom-call | tf_op jit(solution)/shard_map/pallas_call | solution.py:249
  5.1 58.6 %shard_map.38 = (f32[4608,128]{1,0:T(8,128)S(1)}, bf16[16,96,128]{2,1,0:T(8,128)(2,1)S(1)}) custom-call(f32[4608,128]{1,0:T(8,128)S(1)} %shard_map.37.part_ref, bf16[16,96,128]{2,1,0:T(8,128)(2,1)S(1)} %reshape.7.grad_ref), custom_call_target="tpu_custom_call" | custom-call | tf_op jit(solution)/shard_map/pallas_call | solution.py:232
  63.8 0.0 copy-start.1
  63.8 1.4 %copy-done.1 = f32[4608,128]{1,0:T(8,128)} copy-done((f32[4608,128]{1,0:T(8,128)}, f32[4608,128]{1,0:T(8,128)S(1)}, u32[]{:S(2)}) %copy-start.1) | copy-done | bytes 2359320
  65.2 0.9 reshape.8.g_ref
  66.1 33.2 %shard_map.39 = bf16[192,1024]{1,0:T(8,128)(2,1)} custom-call(f32[4608,128]{1,0:T(8,128)} %copy-done.1, bf16[192,1024]{1,0:T(8,128)(2,1)} %reshape.8.g_ref), custom_call_target="tpu_custom_call" | custom-call | tf_op jit(solution)/shard_map/pallas_call | solution.py:405
Async XLA Ops:
  0.0 1.0 %copy-start = (bf16[12,16,1024]{2,1,0:T(8,128)(2,1)S(1)}, bf16[12,16,1024]{2,1,0:T(8,128)(2,1)}, u32[]{:S(2)}) copy-start(bf16[12,16,1024]{2,1,0:T(8,128)(2,1)} %param.4) | copy-start | bytes 1179652
  0.0 2.4 %copy-start.2 = (bf16[1024,1,1024]{2,0,1:T(8,128)(2,1)S(1)}, bf16[1024,1,1024]{2,0,1:T(8,128)(2,1)}, u32[]{:S(2)}) copy-start(bf16[1024,1,1024]{2,0,1:T(8,128)(2,1)} %param.3) | copy-start | bytes 6291460
  63.8 1.4 %copy-start.1 = (f32[4608,128]{1,0:T(8,128)}, f32[4608,128]{1,0:T(8,128)S(1)}, u32[]{:S(2)}) copy-start(f32[4608,128]{1,0:T(8,128)S(1)} %get-tuple-element.7.s_ref) | copy-start | bytes 7077892

commit v3 on v0

v3 whole, which is shorter than its diff:
```python
import functools

import jax
import jax.numpy as jnp
from jax import lax
from jax.experimental import pallas as pl
from jax.experimental.pallas import tpu as pltpu
from jax.sharding import PartitionSpec as P

MESH = pl.DeviceIdType.MESH
F32, BF16 = jnp.float32, jnp.bfloat16
B = 128


def block_rows(i, j):
    return (j * 8 - j * (j - 1) // 2 + (i - j)) * B


def covariance_kernel(act_ref, out_ref):
    for j in range(8):
        column = act_ref[:, j * B : (j + 1) * B]
        part = lax.dot_general(
            act_ref[:, j * B :], column, (((0,), (0,)), ((), ())), preferred_element_type=F32
        )
        out_ref[pl.ds(block_rows(j, j), (8 - j) * B), :] = part


def covariance(act):
    vm = pl.BlockSpec(memory_space=pltpu.VMEM)
    return pl.pallas_call(
        covariance_kernel,
        out_shape=jax.ShapeDtypeStruct((4608, B), F32),
        in_specs=[vm], out_specs=vm,
        compiler_params=pltpu.CompilerParams(vmem_limit_bytes=48 << 20),
    )(act)


def lb(t,j): return jnp.broadcast_to(t[:,j:j+1],(8,128))
def sb(t,r): return jnp.broadcast_to(t[r:r+1,:],(8,128))
def tsum(xs):
    xs=list(xs)
    while len(xs)>1:
        xs=[xs[i]+xs[i+1] if i+1<len(xs) else xs[i] for i in range(0,len(xs),2)]
    return xs[0]
def split(x):
    h=x.astype(BF16); r=x-h.astype(F32); m=r.astype(BF16); l=(r-m.astype(F32)).astype(BF16)
    return h,m,l
def gj(L,R,p,sub,two):
    nv=p//8
    if not two:
        for j in range(p):
            u,r=j//8,j%8
            dinv=1.0/sb(L[u][j],r)
            isr=sub==r
            t=sb(R[u],r)*dinv
            for k in range(j+1,p):
                tk=sb(L[u][k],r)*dinv
                for a in range(nv):
                    y=L[a][k]-L[a][j]*tk
                    L[a][k]=jnp.where(isr,tk,y) if a==u else y
            R=[R[a]-L[a][j]*t for a in range(nv)]
            R[u]=jnp.where(isr,t,R[u])
        return R
    for j in range(0,p,2):
        u,r=j//8,j%8
        a_=sb(L[u][j],r); b_=sb(L[u][j+1],r); c_=sb(L[u][j+1],r+1)
        idet=1.0/(a_*c_-b_*b_)
        p00=c_*idet; p11=a_*idet; p01=b_*idet
        is0=sub==r; is1=sub==r+1
        def upd(cols):
            s0=sb(cols[u],r); s1=sb(cols[u],r+1)
            t0=p00*s0-p01*s1; t1=p11*s1-p01*s0
            out=[cols[a]-(L[a][j]*t0+L[a][j+1]*t1) for a in range(nv)]
            out[u]=jnp.where(is0,t0,jnp.where(is1,t1,out[u]))
            return out
        for k in range(j+2,p):
            o=upd([L[a][k] for a in range(nv)])
            for a in range(nv): L[a][k]=o[a]
        R=upd(R)
    return R
def inv128_ref(X_ref,hook=None,two=False,p=16):
    lane=lax.broadcasted_iota(jnp.int32,(8,128),1)
    sub=lax.broadcasted_iota(jnp.int32,(8,128),0)
    lane_all=lax.broadcasted_iota(jnp.int32,(128,128),1)
    nv=p//8
    G=128//p
    R=[X_ref[8*a:8*a+8,:] for a in range(nv)]
    for g in range(G):
        base=g*p; n=(g+1)%G
        N=[X_ref[n*p+8*a:n*p+8*a+8,:] for a in range(nv)]
        ing=(lane>=base)&(lane<base+p)
        L=[[lb(R[a],base+j) for j in range(p)] for a in range(nv)]
        Rh=[jnp.where(ing,jnp.where(lane-base==sub+8*a,1.0,0.0),R[a]) for a in range(nv)]
        X=X_ref[...]
        h,m,l=split(X)
        LH=jnp.concatenate([h,h,m],axis=1)
        if g<G-1:
            CN=[[lb(N[a],base+j) for j in range(p)] for a in range(nv)]
        T=gj(L,Rh,p,sub,two)
        Tc=jnp.concatenate(T,axis=0)
        if g<G-1:
            Ts=[sb(T[j//8],j%8) for j in range(p)]
            Nn=[jnp.where(ing,0.0,N[a])-tsum([CN[a][j]*Ts[j] for j in range(p)]) for a in range(nv)]
        th,tm,tl=split(Tc)
        def pad(t):
            parts=[]
            if base: parts.append(jnp.zeros((base,128),BF16))
            parts.append(t)
            if base+p<128: parts.append(jnp.zeros((128-base-p,128),BF16))
            return jnp.concatenate(parts,axis=0)
        th,tm,tl=pad(th),pad(tm),pad(tl)
        RH=jnp.concatenate([th,tm,th],axis=0)
        U=jnp.dot(LH,RH,preferred_element_type=F32)
        inga=(lane_all>=base)&(lane_all<base+p)
        Xn=jnp.where(inga,0.0,X)-U
        X_ref[...]=Xn
        X_ref[base:base+p,:]=Tc
        if g<G-1:
            for a in range(nv): X_ref[n*p+8*a:n*p+8*a+8,:]=Nn[a]
            R=Nn
        if hook is not None: hook(g)


def lform(x):
    h,m,l=split(x); return jnp.concatenate([h,h,m,h,l,m],axis=1)
def rform(x):
    h,m,l=split(x); return jnp.concatenate([h,m,h,l,h,m],axis=1)
NT=(((1,),(1,)),((),()))
def nt(a,b): return lax.dot_general(a,b,NT,preferred_element_type=F32)

TOTAL = 4608
FIRST = 1024
H = 896
CA, SA = 112, 56
XB, CB = 448, 56
FH, FC = 512, 32


def step_kernel(tokens, part_ref, grad_ref, out_ref, S, tile, acc, from_core, from_x, za_plus, za_minus, zb_plus, zb_minus, xa,
                acc0, core0, slots0, A, X, G, Mh, Mm, Yh, Ym, MG, s_sem, r_sem, own_sem):
    me = lax.axis_index("bcast")
    column = lax.axis_index("grad")
    core, z, x = me % 2, (me // 2) % 8, me // 16

    def at(c, zz, xx):
        return {"bcast": (xx % 2) * 16 + (zz % 8) * 2 + c}

    twin, up, down, across = at(1 - core, z, x), at(core, z + 1, x), at(core, z + 7, x), at(core, z, x + 1)
    others = [(dz, dx) for dz in (4, 3, 5, 2, 6, 1, 7, 0) for dx in (1, 0) if (dz, dx) != (0, 0)]
    barrier = pltpu.get_barrier_semaphore()
    pl.semaphore_signal(barrier, inc=1, device_id=twin, device_id_type=MESH)
    for dz, dx in others:
        pl.semaphore_signal(barrier, inc=1, device_id=at(core, z + dz, x + dx), device_id_type=MESH)
    for d in range(1, 16):
        pl.semaphore_signal(barrier, inc=1, device_id={"grad": (column + d) % 16}, device_id_type=MESH)
    pl.semaphore_wait(barrier, 31)

    sent = []

    def send(src, dst, to):
        n = len(sent)
        c = pltpu.make_async_remote_copy(src_ref=src, dst_ref=dst, send_sem=s_sem.at[n], recv_sem=r_sem.at[n],
                                         device_id=to, device_id_type=MESH)
        c.start()
        sent.append(c)
        return c

    def ds(start, n):
        return pl.ds(pl.multiple_of(start, 8), n)

    def a_rows(q, h=None):
        return ds((q % 8) * CA + (0 if h is None else h * SA), CA if h is None else SA)

    def b_rows(xx, q=None):
        return ds(H + xx * XB + (0 if q is None else (q % 8) * CB), XB if q is None else CB)

    def pa(c, q, h=None):
        return ds(FIRST + c * H + (q % 8) * CA + (0 if h is None else h * SA), CA if h is None else SA)

    def pb(c, xx, q=None):
        return ds(FIRST + 2 * H + c * H + xx * XB + (0 if q is None else (q % 8) * CB), XB if q is None else CB)

    def mine0(zz, xx):
        return ds(((zz % 8) * 2 + xx % 2) * FC, FC)

    def p0(c, zz, xx):
        return ds(c * FH + ((zz % 8) * 2 + xx % 2) * FC, FC)

    def half0(c):
        return ds(c * FH, FH)

    order = [4, 5, 3, 6, 2, 7, 1, 0]
    swap_0 = send(part_ref.at[half0(1 - core)], core0, twin)
    swap_a = {}

    def swap(d):
        swap_a[d] = send(part_ref.at[pa(1 - core, z + d)], from_core.at[a_rows(z + d)], twin)

    swap(4), swap(5)
    swap_b0 = send(part_ref.at[pb(1 - core, 1 - x)], from_core.at[b_rows(1 - x)], twin)
    for d in order[2:]:
        swap(d)
    swap_b1 = send(part_ref.at[pb(1 - core, x)], from_core.at[b_rows(x)], twin)

    swap_0.wait_recv()
    acc0[...] = part_ref[half0(core)] + core0[...]
    first = [send(acc0.at[mine0(z + dz, x + dx)], slots0.at[dz * 2 + dx], at(core, z + dz, x + dx)) for dz, dx in others]

    def add_a(d):
        swap_a[d].wait_recv()
        acc[a_rows(z + d)] = part_ref[pa(core, z + d)] + from_core[a_rows(z + d)]

    add_a(4)
    ap = [send(acc.at[a_rows(z + 4, h)], za_plus.at[0, h], up) for h in (0, 1)]
    add_a(5)
    am = [send(acc.at[a_rows(z + 5, h)], za_minus.at[0, h], down) for h in (0, 1)]
    swap_b0.wait_recv()
    acc[b_rows(1 - x)] = part_ref[pb(core, 1 - x)] + from_core[b_rows(1 - x)]
    bx = {d: send(acc.at[b_rows(1 - x, z + d)], from_x.at[ds(((z + d) % 8) * CB, CB)], across) for d in order}
    own = pltpu.make_async_copy(grad_ref.at[column], tile.at[column], own_sem)
    own.start()
    tiles = []
    for d in range(1, 16):
        to = (column + d) % 16
        tiles.append(send(grad_ref.at[to], tile.at[column], {"grad": to}))
    for d in order[2:]:
        add_a(d)
    swap_b1.wait_recv()
    acc[b_rows(x)] = part_ref[pb(core, x)] + from_core[b_rows(x)]

    def step_a(s):
        nonlocal ap, am
        q = []
        for h in (0, 1):
            ap[h].wait_recv()
            acc[a_rows(z + 4 - s, h)] += za_plus[s - 1, h]
            if s < 4:
                q.append(send(acc.at[a_rows(z + 4 - s, h)], za_plus.at[s, h], up))
        ap = q
        if s < 4:
            q = []
            for h in (0, 1):
                am[h].wait_recv()
                acc[a_rows(z + 5 + s, h)] += za_minus[s - 1, h]
                if s < 3:
                    q.append(send(acc.at[a_rows(z + 5 + s, h)], za_minus.at[s, h], down))
            am = q

    def take_x(d):
        bx[d].wait_recv()
        acc[b_rows(x, z + d)] += from_x[ds(((z + d) % 8) * CB, CB)]

    bp = bm = None

    def step_b(s):
        nonlocal bp, bm
        if s < 4:
            take_x(4 - s)
        if s:
            bp.wait_recv()
            acc[b_rows(x, z + 4 - s)] += zb_plus[s - 1]
        if s < 4:
            bp = send(acc.at[b_rows(x, z + 4 - s)], zb_plus.at[s], up)
            take_x((5 + s) % 8)
            if s:
                bm.wait_recv()
                acc[b_rows(x, z + 5 + s)] += zb_minus[s - 1]
            if s < 3:
                bm = send(acc.at[b_rows(x, z + 5 + s)], zb_minus.at[s], down)

    def same(rows, to):
        return send(S.at[rows], S.at[rows], to)

    step_a(1)
    step_b(0)
    total = acc0[mine0(z, x)]
    for c, (dz, dx) in zip(first, others):
        c.wait_recv()
        total = total + slots0[dz * 2 + dx]
    S[p0(core, z, x)] = total
    gather0 = [same(p0(core, z, x), at(core, z + dz, x + dx)) for dz, dx in others]
    step_a(2)
    step_b(1)
    step_a(3)
    step_b(2)
    for c in gather0:
        c.wait_recv()
    twin0 = same(half0(core), twin)
    step_a(4)
    xa_c = send(acc.at[a_rows(z, 1 - x)], xa, across)

    def rest():
        nonlocal ap, am, bp, bm
        twins_a, twins_b, xs = [], [], []

        def b_out(q, plus, minus):
            r = pb(core, x, q)
            p = same(r, up) if plus else None
            m = same(r, down) if minus else None
            xs.append((same(r, across), q))
            twins_b.append(same(r, twin))
            return p, m

        def relay():
            c, q = xs.pop(0)
            c.wait_recv()
            twins_b.append(same(pb(core, 1 - x, q), twin))

        step_b(3)
        yield False
        xa_c.wait_recv()
        S[pa(core, z, x)] = acc[a_rows(z, x)] + xa[...]
        xg = same(pa(core, z, x), across)
        yield False
        step_b(4)
        S[pb(core, x, z)] = acc[b_rows(x, z)]
        bp, bm = b_out(z, True, True)
        yield False
        xg.wait_recv()
        r = pa(core, z)
        ap, am = same(r, up), same(r, down)
        twins_a.append(same(r, twin))
        yield False
        for s in range(1, 5):
            bp.wait_recv()
            bp, _ = b_out(z + 8 - s, s < 4, False)
            if s < 4:
                bm.wait_recv()
                _, bm = b_out(z + s, False, s < 3)
            yield False
            ap.wait_recv()
            r = pa(core, z + 8 - s)
            if s < 4:
                ap = same(r, up)
            twins_a.append(same(r, twin))
            if s < 4:
                am.wait_recv()
                r = pa(core, z + s)
                if s < 3:
                    am = same(r, down)
                twins_a.append(same(r, twin))
            yield False
        for c in twins_a:
            c.wait_recv()
        yield True
        while xs:
            relay()
            if xs:
                relay()
            yield True
        for c in twins_b:
            c.wait_recv()
        yield True

    work = rest()

    def advance():
        return next(work, True)

    scale = 1.0 / tokens
    eye = jnp.where(lax.broadcasted_iota(jnp.int32, (B, B), 0) == lax.broadcasted_iota(jnp.int32, (B, B), 1), 1.0, 0.0).astype(F32)
    K = 3 * B

    def take(j):
        d, n = block_rows(j, j), (8 - j) * B
        diagonal, below = S[d : d + B, :] * scale + eye, S[d + B : d + n, :] * scale if n > B else None
        if j:
            diagonal = diagonal + A[d : d + B, :]
            below = below + A[d + B : d + n, :] if n > B else None
        X[...] = diagonal
        if n > B:
            A[d + B : d + n, :] = below

    def body(j):
        R, c = (7 - j) * B, block_rows(j, j) + B
        dcat = rform(X[...])
        mg = nt(lform(G[:, j * B : (j + 1) * B])[:, :K], dcat[:, :K])
        MG[:, j * B : (j + 1) * B] = mg
        if R:
            ccat = lform(A[c : c + R, :])[:, :K]
            mcat = rform(nt(ccat, dcat[:, :K]))[:, :K]
            Mh[c : c + R, :] = mcat[:, 0:B]
            Mm[c : c + R, :] = mcat[:, B : 2 * B]
            for k in range(j + 1, 8):
                o, rk, n = (k - j - 1) * B, block_rows(k, k), (8 - k) * B
                u = nt(mcat[o:R], ccat[o : o + B])
                A[rk : rk + n, :] = A[rk : rk + n, :] - u if j else -u
            G[:, (j + 1) * B :] -= nt(rform(mg)[:, :K], ccat)

    twin0.wait_recv()
    take(0)

    def hook0(g):
        if g in (1, 5, 6):
            advance()

    inv128_ref(X, hook0)
    for c in tiles:
        c.wait_recv()
    own.wait()
    rows = out_ref.shape[0] // 16
    for n in range(16):
        G[n * rows : (n + 1) * rows, :] = tile[n].astype(F32)[:rows, :]
    advance()
    body(0)
    while not advance():
        pass
    take(1)

    def hook1(g):
        advance()

    inv128_ref(X, hook1)
    body(1)
    for _ in range(12):
        advance()
    for c in sent:
        c.wait_send()
    take(2)

    def later(j, carry):
        inv128_ref(X)
        for jj in range(2, 8):

            @pl.when(j == jj)
            def _():
                body(jj)
                if jj < 7:
                    take(jj + 1)

        return carry

    lax.fori_loop(2, 8, later, 0)
    for j in range(7, -1, -1):
        y = MG[:, j * B : (j + 1) * B]
        if j < 7:
            c, R = block_rows(j, j) + B, (7 - j) * B
            yh, ym = Yh[:, (j + 1) * B :], Ym[:, (j + 1) * B :]
            mh, mm = Mh[c : c + R, :], Mm[c : c + R, :]
            y = y - (jnp.dot(yh, mh, preferred_element_type=F32) + jnp.dot(yh, mm, preferred_element_type=F32)
                     + jnp.dot(ym, mh, preferred_element_type=F32))
        h = y.astype(BF16)
        Yh[:, j * B : (j + 1) * B] = h
        Ym[:, j * B : (j + 1) * B] = (y - h.astype(F32)).astype(BF16)
        out_ref[:, j * B : (j + 1) * B] = h


N_COPIES = 176


def step(part, grads, rows, tokens):
    dma = pltpu.SemaphoreType.DMA
    vm = pl.BlockSpec(memory_space=pltpu.VMEM)
    n = 16 * rows
    return pl.pallas_call(
        functools.partial(step_kernel, tokens),
        out_shape=jax.ShapeDtypeStruct((n, 1024), BF16),
        in_specs=[vm, vm],
        out_specs=vm,
        scratch_shapes=[
            pltpu.VMEM((TOTAL, B), F32), pltpu.VMEM(grads.shape, BF16),
            pltpu.VMEM((2 * H, B), F32), pltpu.VMEM((2 * H, B), F32), pltpu.VMEM((XB, B), F32),
            pltpu.VMEM((4, 2, SA, B), F32), pltpu.VMEM((3, 2, SA, B), F32),
            pltpu.VMEM((4, CB, B), F32), pltpu.VMEM((3, CB, B), F32), pltpu.VMEM((SA, B), F32),
            pltpu.VMEM((FH, B), F32), pltpu.VMEM((FH, B), F32), pltpu.VMEM((16, FC, B), F32),
            pltpu.VMEM((TOTAL, B), F32), pltpu.VMEM((B, B), F32), pltpu.VMEM((n, 1024), F32),
            pltpu.VMEM((TOTAL, B), BF16), pltpu.VMEM((TOTAL, B), BF16),
            pltpu.VMEM((n, 1024), BF16), pltpu.VMEM((n, 1024), BF16), pltpu.VMEM((n, 1024), F32),
            dma((N_COPIES,)), dma((N_COPIES,)), dma,
        ],
        compiler_params=pltpu.CompilerParams(collective_id=0, has_side_effects=True, vmem_limit_bytes=56 << 20),
    )(part, grads)


def per_device(activations, gradient, block_map):
    tokens = activations.shape[0] * lax.axis_size("bcast")
    rows = gradient.shape[0]
    part = covariance(activations[:, 0, :])
    chooser = (block_map[None, :] == jnp.arange(16, dtype=jnp.int32)[:, None]).astype(BF16)
    ordered = jnp.einsum("kj,rjb->krb", chooser, gradient, preferred_element_type=F32).astype(BF16)
    ordered = jnp.pad(ordered, ((0, 0), (0, -rows % 16), (0, 0)))
    return step(part, ordered, rows, tokens)[:, None, :]


def solution(mesh):
    return jax.shard_map(
        per_device,
        mesh=mesh,
        in_specs=(P("bcast", "grad", None), P(("bcast", "grad"), None, None), P()),
        out_specs=P("bcast", "grad", None),
        check_vma=False,
    )
```

time: 875 us -> 103 us (0.12)
  waiting for transfers between devices: 836 us -> 0 us
  Pallas kernels: 0 us -> 96.9 us
  between operations: 14.9 us -> 0.04 us
  matrix products: 12.6 us -> 0.9 us
    psum x2 -> x0, waiting for transfers between devices: 835 us -> none  [the longest x1 590 us: spread(): return lax.psum(block, axis)]
    pallas_call x0 -> x2, Pallas kernels: none -> 96.9 us  [the longest x1 94.3 us: step(): pl.pallas_call(functools.partial(step_kernel, tokens), out_shape=jax.Shap...]
    dot_general x3 -> x1, matrix products: 12.6 us -> 0.9 us  [per_device(): jnp.einsum('kj,rjb->krb', chooser, gradient, preferred_element_type=F32)]
  transfers between devices with their start and end apart: 3 -> 0, of which waited for: 2 -> 0; matrix products, arithmetic and copies ran while one was open for 1% -> 0% of each run, Pallas kernels for 0% -> 0%
where the time goes in v3:
time: 103 us
  Pallas kernels  96.9 us (94%)
  local copies, waits for them, and re-layouts  5.28 us (5%)
    pallas_call x1, Pallas kernels, step(): pl.pallas_call(functools.partial(step_kernel, tokens), out_shape=jax.Shap...  94.3 us
    unnamed x7, local copies, waits for them, and re-layouts  4.17 us
    pallas_call x1, Pallas kernels, covariance(): pl.pallas_call(covariance_kernel, out_shape=jax.ShapeDtypeStruct((4608, B...  2.69 us

profile of v3, /device:TPU:1, one launch (start us, length us, event | category | flops | bytes accessed | tf_op | source)
XLA Modules:
  0.0 103.2 jit_solution(15505547344860936195)
XLA Ops:
  0.0 0.0 copy-start
  0.0 0.0 copy-start.2
  0.0 1.0 copy-done
  1.0 0.9 convolution_convert_fusion
  1.9 0.2 copy.5
  2.1 0.9 pad.4.grad_ref
  3.0 0.0 copy-done.2
  3.0 2.7 %shard_map.37.part_ref = f32[4608,128]{1,0:T(8,128)S(1)} custom-call(bf16[1024,1024]{1,0:T(8,128)(2,1)S(1)} %bitcast.6), custom_call_target="tpu_custom_call" | custom-call | tf_op jit(solution)/shard_map/pallas_call | solution.py:30
  5.7 0.0 copy-start.1
  5.7 1.4 %copy-done.1 = f32[4608,128]{1,0:T(8,128)} copy-done((f32[4608,128]{1,0:T(8,128)}, f32[4608,128]{1,0:T(8,128)S(1)}, u32[]{:S(2)}) %copy-start.1) | copy-done | bytes 2359320
  7.1 94.3 %shard_map.38 = bf16[192,1024]{1,0:T(8,128)(2,1)} custom-call(f32[4608,128]{1,0:T(8,128)} %copy-done.1, bf16[16,16,1024]{2,1,0:T(8,128)(2,1)} %pad.4.grad_ref), custom_call_target="tpu_custom_call" | custom-call | tf_op jit(solution)/shard_map/pallas_call | solution.py:455
  101.4 1.8 %copy.7 = bf16[192,1,1024]{2,0,1:T(8,128)(2,1)} copy(bf16[192,1,1024]{2,0,1:T(8,128)(2,1)} %bitcast.7) | data formatting | bytes 786432
Async XLA Ops:
  0.0 1.0 copy-start
  0.0 3.0 %copy-start.2 = (bf16[1024,1,1024]{2,0,1:T(8,128)(2,1)S(1)}, bf16[1024,1,1024]{2,0,1:T(8,128)(2,1)}, u32[]{:S(2)}) copy-start(bf16[1024,1,1024]{2,0,1:T(8,128)(2,1)} %param.3) | copy-start | bytes 6291460
  5.7 1.4 %copy-start.1 = (f32[4608,128]{1,0:T(8,128)}, f32[4608,128]{1,0:T(8,128)S(1)}, u32[]{:S(2)}) copy-start(f32[4608,128]{1,0:T(8,128)S(1)} %shard_map.37.part_ref) | copy-start | bytes 7077892

commit v4 on v2

--- a/solution.py
+++ b/solution.py
@@ -96,12 +96,6 @@
     swap_b0.wait_recv()
     acc[b_rows(1 - x)] = part_ref[pb(core, 1 - x)] + from_core[b_rows(1 - x)]
     bx = {d: send(acc.at[b_rows(1 - x, z + d)], from_x.at[ds(((z + d) % 8) * CB, CB)], across) for d in order}
-    own = pltpu.make_async_copy(grad_ref.at[column], tile_ref.at[column], own_sem)
-    own.start()
-    tiles = []
-    for d in range(1, 16):
-        to = (column + d) % 16
-        tiles.append(send(grad_ref.at[to], tile_ref.at[column], {"grad": to}))
     for d in order[2:]:
         add_a(d)
     swap_b1.wait_recv()
@@ -160,6 +154,12 @@
     step_b(1)
     step_a(3)
     step_b(2)
+    own = pltpu.make_async_copy(grad_ref.at[column], tile_ref.at[column], own_sem)
+    own.start()
+    tiles = []
+    for d in range(1, 16):
+        to = (column + d) % 16
+        tiles.append(send(grad_ref.at[to], tile_ref.at[column], {"grad": to}))
     step_a(4)
     xa_c = send(acc.at[a_rows(z, 1 - x)], xa, across)
     step_b(3)
@@ -240,7 +240,7 @@
             pltpu.VMEM((4, 72, B), F32), pltpu.VMEM((3, 72, B), F32), pltpu.VMEM((72, B), F32),
             dma((N_COPIES,)), dma((N_COPIES,)), dma,
         ],
-        compiler_params=pltpu.CompilerParams(collective_id=0, has_side_effects=True, vmem_limit_bytes=48 << 20),
+        compiler_params=pltpu.CompilerParams(collective_id=0, has_side_effects=True, vmem_limit_bytes=18 << 20),
     )(part, grads)
 
 
@@ -250,144 +250,142 @@
         covariance_kernel,
         out_shape=jax.ShapeDtypeStruct((4608, B), F32),
         in_specs=[vm], out_specs=vm,
-        compiler_params=pltpu.CompilerParams(vmem_limit_bytes=48 << 20),
+        compiler_params=pltpu.CompilerParams(vmem_limit_bytes=20 << 20),
     )(act)
 
 
-def lb(t,j): return jnp.broadcast_to(t[:,j:j+1],(8,128))
-def sb(t,r): return jnp.broadcast_to(t[r:r+1,:],(8,128))
+def lb(t, j):
+    return jnp.broadcast_to(t[:, j : j + 1], (8, B))
+
+
+def sb(t, r):
+    return jnp.broadcast_to(t[r : r + 1, :], (8, B))
+
+
 def tsum(xs):
-    xs=list(xs)
-    while len(xs)>1:
-        xs=[xs[i]+xs[i+1] if i+1<len(xs) else xs[i] for i in range(0,len(xs),2)]
+    xs = list(xs)
+    while len(xs) > 1:
+        xs = [xs[i] + xs[i + 1] if i + 1 < len(xs) else xs[i] for i in range(0, len(xs), 2)]
     return xs[0]
-def split(x):
-    h=x.astype(BF16); r=x-h.astype(F32); m=r.astype(BF16); l=(r-m.astype(F32)).astype(BF16)
-    return h,m,l
-def gj(L,R,p,sub,two):
-    nv=p//8
-    if not two:
-        for j in range(p):
-            u,r=j//8,j%8
-            dinv=1.0/sb(L[u][j],r)
-            isr=sub==r
-            t=sb(R[u],r)*dinv
-            for k in range(j+1,p):
-                tk=sb(L[u][k],r)*dinv
-                for a in range(nv):
-                    y=L[a][k]-L[a][j]*tk
-                    L[a][k]=jnp.where(isr,tk,y) if a==u else y
-            R=[R[a]-L[a][j]*t for a in range(nv)]
-            R[u]=jnp.where(isr,t,R[u])
-        return R
-    for j in range(0,p,2):
-        u,r=j//8,j%8
-        a_=sb(L[u][j],r); b_=sb(L[u][j+1],r); c_=sb(L[u][j+1],r+1)
-        idet=1.0/(a_*c_-b_*b_)
-        p00=c_*idet; p11=a_*idet; p01=b_*idet
-        is0=sub==r; is1=sub==r+1
-        def upd(cols):
-            s0=sb(cols[u],r); s1=sb(cols[u],r+1)
-            t0=p00*s0-p01*s1; t1=p11*s1-p01*s0
-            out=[cols[a]-(L[a][j]*t0+L[a][j+1]*t1) for a in range(nv)]
-            out[u]=jnp.where(is0,t0,jnp.where(is1,t1,out[u]))
-            return out
-        for k in range(j+2,p):
-            o=upd([L[a][k] for a in range(nv)])
-            for a in range(nv): L[a][k]=o[a]
-        R=upd(R)
+
+NT=(((1,),(1,)),((),()))
+def nt(a,b): return lax.dot_general(a,b,NT,preferred_element_type=F32)
+def split2(x):
+    h=x.astype(BF16); return h,(x-h.astype(F32)).astype(BF16)
+def lform3(x):
+    h,m=split2(x); return jnp.concatenate([h,h,m],axis=1)
+def rform3(x):
+    h,m=split2(x); return jnp.concatenate([h,m,h],axis=1)
+def gj(L, R, sub):
+    for j in range(16):
+        u, r = j // 8, j % 8
+        dinv = 1.0 / sb(L[u][j], r)
+        isr = sub == r
+        t = sb(R[u], r) * dinv
+        for k in range(j + 1, 16):
+            tk = sb(L[u][k], r) * dinv
+            for a in range(2):
+                y = L[a][k] - L[a][j] * tk
+                L[a][k] = jnp.where(isr, tk, y) if a == u else y
+        R = [R[a] - L[a][j] * t for a in range(2)]
+        R[u] = jnp.where(isr, t, R[u])
     return R
-def inv128_ref(X_ref,two=False,p=16):
+
+
+def inv128_h(X_ref,hook=None,p=16):
     lane=lax.broadcasted_iota(jnp.int32,(8,128),1)
     sub=lax.broadcasted_iota(jnp.int32,(8,128),0)
     lane_all=lax.broadcasted_iota(jnp.int32,(128,128),1)
-    nv=p//8
-    G=128//p
+    nv=p//8; Gn=128//p
     R=[X_ref[8*a:8*a+8,:] for a in range(nv)]
-    for g in range(G):
-        base=g*p; n=(g+1)%G
+    for g in range(Gn):
+        base=g*p; n=(g+1)%Gn
         N=[X_ref[n*p+8*a:n*p+8*a+8,:] for a in range(nv)]
         ing=(lane>=base)&(lane<base+p)
         L=[[lb(R[a],base+j) for j in range(p)] for a in range(nv)]
         Rh=[jnp.where(ing,jnp.where(lane-base==sub+8*a,1.0,0.0),R[a]) for a in range(nv)]
         X=X_ref[...]
-        h,m,l=split(X)
+        h,m=split2(X)
         LH=jnp.concatenate([h,h,m],axis=1)
-        if g<G-1:
-            CN=[[lb(N[a],base+j) for j in range(p)] for a in range(nv)]
-        T=gj(L,Rh,p,sub,two)
+        if g<Gn-1: CN=[[lb(N[a],base+j) for j in range(p)] for a in range(nv)]
+        if hook is not None: hook(g)
+        T=gj(L,Rh,sub)
         Tc=jnp.concatenate(T,axis=0)
-        if g<G-1:
+        if g<Gn-1:
             Ts=[sb(T[j//8],j%8) for j in range(p)]
             Nn=[jnp.where(ing,0.0,N[a])-tsum([CN[a][j]*Ts[j] for j in range(p)]) for a in range(nv)]
-        th,tm,tl=split(Tc)
+        th,tm=split2(Tc)
         def pad(t):
             parts=[]
             if base: parts.append(jnp.zeros((base,128),BF16))
             parts.append(t)
             if base+p<128: parts.append(jnp.zeros((128-base-p,128),BF16))
             return jnp.concatenate(parts,axis=0)
-        th,tm,tl=pad(th),pad(tm),pad(tl)
-        RH=jnp.concatenate([th,tm,th],axis=0)
-        U=jnp.dot(LH,RH,preferred_element_type=F32)
+        th,tm=pad(th),pad(tm)
+        U=jnp.dot(LH,jnp.concatenate([th,tm,th],axis=0),preferred_element_type=F32)
         inga=(lane_all>=base)&(lane_all<base+p)
-        Xn=jnp.where(inga,0.0,X)-U
-        X_ref[...]=Xn
+        X_ref[...]=jnp.where(inga,0.0,X)-U
         X_ref[base:base+p,:]=Tc
-        if g<G-1:
+        if g<Gn-1:
             for a in range(nv): X_ref[n*p+8*a:n*p+8*a+8,:]=Nn[a]
             R=Nn
-
-
-def lform(x):
-    h,m,l=split(x); return jnp.concatenate([h,h,m,h,l,m],axis=1)
-def rform(x):
-    h,m,l=split(x); return jnp.concatenate([h,m,h,l,h,m],axis=1)
-NT=(((1,),(1,)),((),()))
-def nt(a,b): return lax.dot_general(a,b,NT,preferred_element_type=F32)
-def factor_kernel(unroll,KA,KG,tokens,s_ref,g_ref,o_ref,A,X,G,Mh,Mm,Yh,Ym,MG):
+def factor_kernel(tokens,s_ref,g_ref,o_ref,A,X0,X1,G,Mh,Mm,Yh,Ym,MG):
     eye=jnp.where(lax.broadcasted_iota(jnp.int32,(B,B),0)==lax.broadcasted_iota(jnp.int32,(B,B),1),1.0,0.0).astype(F32)
     scale=1.0/tokens
+    Xs=(X0,X1)
+    def cov(r,n): return s_ref[r:r+n,:]*scale
+    X0[...]=cov(0,B)+eye
+    def start(g):
+        rows=G.shape[0]//16
+        for i in (2*g,2*g+1): G[i*rows:(i+1)*rows,:]=g_ref[i].astype(F32)[:rows,:]
+    hook=start
     for j in range(8):
-        for i in range(j,8):
-            r=block_rows(i,j)
-            v=s_ref[r:r+B,:]*scale
-            A[r:r+B,:]=v+eye if i==j else v
-    G[...]=g_ref[...].astype(F32)
-    def body(j):
-        R=(7-j)*B; d=block_rows(j,j); c=d+B
-        dcat=rform(X[...])
-        gl=lform(G[:,j*B:(j+1)*B])
-        mg=nt(gl[:,:KG],dcat[:,:KG])
-        MG[:,j*B:(j+1)*B]=mg
+        X,Xn=Xs[j%2],Xs[1-j%2]
+        inv128_h(X,hook)
+        R=(7-j)*B; c=block_rows(j,j)+B
+        dcat=rform3(X[...])
+        jobs=[]
         if R:
-            col=A[c:c+R,:]
-            ccat=lform(col)
-            m=nt(ccat[:,:KA],dcat[:,:KA])
-            mcat=rform(m)
-            Mh[c:c+R,:]=mcat[:,0:B]; Mm[c:c+R,:]=mcat[:,B:2*B]
-            for k in range(j+1,8):
-                o=(k-j-1)*B
-                rk=block_rows(k,k); n=(8-k)*B
-                A[rk:rk+n,:]-=nt(mcat[o:R,:KA],ccat[o:o+B,:KA])
-            gm=rform(mg)
-            G[:,(j+1)*B:]-=nt(gm[:,:KG],ccat[:,:KG])
-    if unroll:
-        for j in range(8):
-            d=block_rows(j,j)
-            X[...]=A[d:d+B,:]
-            inv128_ref(X)
-            body(j)
-    else:
-        def it(j,carry):
-            d=pl.multiple_of((j*8-j*(j-1)//2)*B,B)
-            X[...]=A[pl.ds(d,B),:]
-            inv128_ref(X)
-            for jj in range(8):
-                @pl.when(j==jj)
-                def _(): body(jj)
-            return carry
-        lax.fori_loop(0,8,it,0)
+            col=cov(c,R) if j==0 else A[c:c+R,:]
+            ccat=lform3(col)
+            m1=rform3(nt(ccat[0:B],dcat))
+            rk=block_rows(j+1,j+1)
+            old=(cov(rk,B)+eye) if j==0 else A[rk:rk+B,:]
+            Xn[...]=old-nt(m1,ccat[0:B])
+            st={}
+            def j0(j=j,R=R,c=c,ccat=ccat,dcat=dcat,m1=m1,st=st):
+                mcat=m1 if R==B else jnp.concatenate([m1,rform3(nt(ccat[B:R],dcat))],axis=0)
+                st['m']=mcat
+                Mh[c:c+R,:]=mcat[:,0:B]; Mm[c:c+R,:]=mcat[:,B:2*B]
+            def j1(j=j,R=R,ccat=ccat,dcat=dcat,st=st):
+                mg=nt(lform3(G[:,j*B:(j+1)*B]),dcat)
+                MG[:,j*B:(j+1)*B]=mg
+                st['g']=rform3(mg)
+            jobs=[j0,j1]
+            def tr(k,j=j,R=R,ccat=ccat,st=st):
+                o=(k-j-1)*B; rk=block_rows(k,k); n=(8-k)*B
+                if k==j+1: o2,rk,n=o+B,rk+B,n-B
+                else: o2=o
+                if n:
+                    u=nt(st['m'][o2:R],ccat[o:o+B])
+                    if j==0:
+                        v=cov(rk,n)-u
+                        if k!=j+1:
+                            A[rk:rk+B,:]=v[0:B]+eye
+                            if n>B: A[rk+B:rk+n,:]=v[B:]
+                        else: A[rk:rk+n,:]=v
+                    else: A[rk:rk+n,:]-=u
+            def gu(lo,hi,j=j,ccat=ccat,st=st):
+                if hi>lo: G[:,(j+1)*B+lo*B:(j+1)*B+hi*B]-=nt(st['g'],ccat[lo*B:hi*B])
+            nk=7-j
+            for k in range(j+1,8): jobs.append(functools.partial(tr,k))
+            jobs.append(functools.partial(gu,0,nk//2)); jobs.append(functools.partial(gu,nk//2,nk))
+        else:
+            MG[:,j*B:]=nt(lform3(G[:,j*B:]),dcat)
+        per=[[] for _ in range(8)]
+        for i,jb in enumerate(jobs): per[min(7,i*8//max(1,len(jobs)))].append(jb)
+        def hook(g,per=per):
+            for jb in per[g]: jb()
     for j in range(7,-1,-1):
         y=MG[:,j*B:(j+1)*B]
         if j<7:
@@ -399,14 +397,14 @@
         Yh[:,j*B:(j+1)*B]=h
         Ym[:,j*B:(j+1)*B]=(y-h.astype(F32)).astype(BF16)
         o_ref[:,j*B:(j+1)*B]=h
-def factor(s,g,tokens,unroll=False,KA=384,KG=384):
+def factor(s,g,rows,tokens):
     vm=pl.BlockSpec(memory_space=pltpu.VMEM)
-    n=g.shape[0]
-    return pl.pallas_call(functools.partial(factor_kernel,unroll,KA,KG,tokens),
+    n=16*rows
+    return pl.pallas_call(functools.partial(factor_kernel,tokens),
       out_shape=jax.ShapeDtypeStruct((n,1024),BF16),in_specs=[vm,vm],out_specs=vm,
-      scratch_shapes=[pltpu.VMEM((4608,B),F32),pltpu.VMEM((B,B),F32),pltpu.VMEM((n,1024),F32),pltpu.VMEM((4608,B),BF16),pltpu.VMEM((4608,B),BF16),
+      scratch_shapes=[pltpu.VMEM((4608,B),F32),pltpu.VMEM((B,B),F32),pltpu.VMEM((B,B),F32),pltpu.VMEM((n,1024),F32),pltpu.VMEM((4608,B),BF16),pltpu.VMEM((4608,B),BF16),
         pltpu.VMEM((n,1024),BF16),pltpu.VMEM((n,1024),BF16),pltpu.VMEM((n,1024),F32)],
-      compiler_params=pltpu.CompilerParams(vmem_limit_bytes=56<<20))(s,g)
+      compiler_params=pltpu.CompilerParams(vmem_limit_bytes=28<<20))(s,g)
 
 
 def per_device(activations, gradient, block_map):
@@ -414,9 +412,10 @@
     rows = gradient.shape[0]
     part = covariance(activations[:, 0, :])
     chooser = (block_map[None, :] == jnp.arange(16, dtype=jnp.int32)[:, None]).astype(BF16)
-    ordered = jnp.einsum("kj,rjb->krb", chooser, gradient, preferred_element_type=F32).astype(BF16)
-    total, tiles = exchange(part, ordered.reshape(16, rows * 8, 128))
-    return factor(total, tiles.reshape(16 * rows, 1024), tokens)[:, None, :]
+    padded = jnp.pad(gradient, ((0, -rows % 16), (0, 0), (0, 0)))
+    ordered = jnp.einsum("kj,rjb->krb", chooser, padded, preferred_element_type=F32).astype(BF16)
+    total, tiles = exchange(part, ordered)
+    return factor(total, tiles, rows, tokens)[:, None, :]
 
 
 def solution(mesh):

time: 99.5 us -> 93.5 us (0.940)
  Pallas kernels: 94.5 us -> 90.1 us
  local copies, waits for them, and re-layouts: 3.83 us -> 1.88 us
    pallas_call x1, Pallas kernels: 33.2 us -> 27.8 us  [factor(): pl.pallas_call(functools.partial(factor_kernel, tokens), out_shape=jax.Sh...]
    reshape x2 -> x0, local copies, waits for them, and re-layouts: 1.19 us -> none  [the longest x1 0.91 us: per_device(): return factor(total, tiles.reshape(16 * rows, 1024), tokens)[:, None, :]]
    unnamed x6 -> x2, local copies, waits for them, and re-layouts: 2.41 us -> 1.59 us
where the time goes in v4:
time: 93.5 us; the launch traced here: 93.3 us
  Pallas kernels  90.1 us (96%)
  local copies, waits for them, and re-layouts  1.88 us (2%)
  matrix products  1.27 us (1%)
    pallas_call x1, Pallas kernels, exchange(): pl.pallas_call(exchange_body, out_shape=(jax.ShapeDtypeStruct((4608, B),...  59.6 us
    pallas_call x1, Pallas kernels, factor(): pl.pallas_call(functools.partial(factor_kernel, tokens), out_shape=jax.Sh...  27.8 us
    pallas_call x1, Pallas kernels, covariance(): pl.pallas_call(covariance_kernel, out_shape=jax.ShapeDtypeStruct((4608, B...  2.69 us

profile of v4, /device:TPU:1, one launch (start us, length us, event | category | flops | bytes accessed | tf_op | source)
XLA Modules:
  0.0 93.3 jit_solution(4528106460925937294)
XLA Ops:
  0.0 1.3 %fusion = bf16[16,16,1024]{2,0,1:T(8,128)(2,1)S(1)} fusion(bf16[12,16,1024]{2,1,0:T(8,128)(2,1)} %param.4, s32[16]{0:T(128)} %param.5), kind=kOutput, calls=%fused_computation.1 | convolution fusion | flops 8388864 | bytes 917568 | tf_op jit(solution)/shard_map/kj,rjb->krb/dot_general | solution.py:416
  1.3 0.3 copy.6.grad_ref
  1.6 0.0 copy-start
  1.6 1.6 %copy-done = bf16[1024,1,1024]{2,0,1:T(8,128)(2,1)S(1)} copy-done((bf16[1024,1,1024]{2,0,1:T(8,128)(2,1)S(1)}, bf16[1024,1,1024]{2,0,1:T(8,128)(2,1)}, u32[]{:S(2)}) %copy-start) | copy-done | bytes 2097176
  3.2 2.7 %shard_map.37.part_ref = f32[4608,128]{1,0:T(8,128)S(1)} custom-call(bf16[1024,1024]{1,0:T(8,128)(2,1)S(1)} %bitcast.5), custom_call_target="tpu_custom_call" | custom-call | tf_op jit(solution)/shard_map/pallas_call | solution.py:249
  5.9 59.6 %shard_map.38 = (f32[4608,128]{1,0:T(8,128)S(1)}, bf16[16,16,1024]{2,1,0:T(8,128)(2,1)S(1)}) custom-call(f32[4608,128]{1,0:T(8,128)S(1)} %shard_map.37.part_ref, bf16[16,16,1024]{2,1,0:T(8,128)(2,1)S(1)} %copy.6.grad_ref), custom_call_target="tpu_custom_call" | custom-call | tf_op jit(solution)/shard_map/pallas_call | solution.py:232
  65.5 27.8 %shard_map.39 = bf16[192,1024]{1,0:T(8,128)(2,1)} custom-call(f32[4608,128]{1,0:T(8,128)S(1)} %get-tuple-element.7.s_ref, bf16[16,16,1024]{2,1,0:T(8,128)(2,1)S(1)} %get-tuple-element.8.g_ref), custom_call_target="tpu_custom_call" | custom-call | tf_op jit(solution)/shard_map/pallas_call | solution.py:403
Async XLA Ops:
  1.6 1.6 %copy-start = (bf16[1024,1,1024]{2,0,1:T(8,128)(2,1)S(1)}, bf16[1024,1,1024]{2,0,1:T(8,128)(2,1)}, u32[]{:S(2)}) copy-start(bf16[1024,1,1024]{2,0,1:T(8,128)(2,1)} %param.3) | copy-start | bytes 6291460

commit v5 on v4

--- a/solution.py
+++ b/solution.py
@@ -109,6 +109,8 @@
             acc[a_rows(z + 4 - s, h)] += za_plus[s - 1, h]
             if s < 4:
                 q.append(send(acc.at[a_rows(z + 4 - s, h)], za_plus.at[s, h], up))
+            else:
+                q.append(send(acc.at[a_rows(z, h)], xa.at[h], across))
         ap = q
         if s < 4:
             q = []
@@ -161,17 +163,11 @@
         to = (column + d) % 16
         tiles.append(send(grad_ref.at[to], tile_ref.at[column], {"grad": to}))
     step_a(4)
-    xa_c = send(acc.at[a_rows(z, 1 - x)], xa, across)
     step_b(3)
-    xa_c.wait_recv()
-    sum_ref[pa(core, z, x)] = acc[a_rows(z, x)] + xa[...]
 
     def same(rows, to):
         return send(sum_ref.at[rows], sum_ref.at[rows], to)
 
-    xg = same(pa(core, z, x), across)
-    step_b(4)
-    sum_ref[pb(core, x, z)] = acc[b_rows(x, z)]
     twins, xs = [], []
 
     def b_out(q, plus, minus):
@@ -182,11 +178,16 @@
         twins.append(same(r, twin))
         return p, m
 
+    across_a, ap, am = ap, [None, None], [None, None]
+    for h in (0, 1):
+        across_a[h].wait_recv()
+        r = pa(core, z, h)
+        sum_ref[r] = acc[a_rows(z, h)] + xa[h]
+        ap[h], am[h] = same(r, up), same(r, down)
+        twins.append(same(r, twin))
+    step_b(4)
+    sum_ref[pb(core, x, z)] = acc[b_rows(x, z)]
     bp, bm = b_out(z, True, True)
-    xg.wait_recv()
-    r = pa(core, z)
-    ap, am = same(r, up), same(r, down)
-    twins.append(same(r, twin))
 
     def relay():
         c, q = xs.pop(0)
@@ -194,22 +195,23 @@
         twins.append(same(pb(core, 1 - x, q), twin))
 
     for s in range(1, 5):
+        for h in (0, 1):
+            ap[h].wait_recv()
+            r = pa(core, z + 8 - s, h)
+            if s < 4:
+                ap[h] = same(r, up)
+            twins.append(same(r, twin))
+            if s < 4:
+                am[h].wait_recv()
+                r = pa(core, z + s, h)
+                if s < 3:
+                    am[h] = same(r, down)
+                twins.append(same(r, twin))
         bp.wait_recv()
         bp, _ = b_out(z + 8 - s, s < 4, False)
         if s < 4:
             bm.wait_recv()
             _, bm = b_out(z + s, False, s < 3)
-        ap.wait_recv()
-        r = pa(core, z + 8 - s)
-        if s < 4:
-            ap = same(r, up)
-        twins.append(same(r, twin))
-        if s < 4:
-            am.wait_recv()
-            r = pa(core, z + s)
-            if s < 3:
-                am = same(r, down)
-            twins.append(same(r, twin))
         relay()
         if s > 1:
             relay()
@@ -237,7 +239,7 @@
         scratch_shapes=[
             pltpu.VMEM((2304, B), F32), pltpu.VMEM((2304, B), F32), pltpu.VMEM((576, B), F32),
             pltpu.VMEM((4, 2, 72, B), F32), pltpu.VMEM((3, 2, 72, B), F32),
-            pltpu.VMEM((4, 72, B), F32), pltpu.VMEM((3, 72, B), F32), pltpu.VMEM((72, B), F32),
+            pltpu.VMEM((4, 72, B), F32), pltpu.VMEM((3, 72, B), F32), pltpu.VMEM((2, 72, B), F32),
             dma((N_COPIES,)), dma((N_COPIES,)), dma,
         ],
         compiler_params=pltpu.CompilerParams(collective_id=0, has_side_effects=True, vmem_limit_bytes=18 << 20),

time: 93.5 us -> 94.1 us (level)
  no operation moved by 1% of the time
where the time goes in v5:
time: 94.1 us; the launch traced here: 93.9 us
  Pallas kernels  90.8 us (96%)
  local copies, waits for them, and re-layouts  1.88 us (2%)
  matrix products  1.27 us (1%)
    pallas_call x1, Pallas kernels, exchange(): pl.pallas_call(exchange_body, out_shape=(jax.ShapeDtypeStruct((4608, B),...  60.2 us
    pallas_call x1, Pallas kernels, factor(): pl.pallas_call(functools.partial(factor_kernel, tokens), out_shape=jax.Sh...  27.8 us
    pallas_call x1, Pallas kernels, covariance(): pl.pallas_call(covariance_kernel, out_shape=jax.ShapeDtypeStruct((4608, B...  2.69 us

profile of v5, /device:TPU:1, one launch (start us, length us, event | category | flops | bytes accessed | tf_op | source)
XLA Modules:
  0.0 93.9 jit_solution(11858582192257444440)
XLA Ops:
  0.0 1.3 %fusion = bf16[16,16,1024]{2,0,1:T(8,128)(2,1)S(1)} fusion(bf16[12,16,1024]{2,1,0:T(8,128)(2,1)} %param.4, s32[16]{0:T(128)} %param.5), kind=kOutput, calls=%fused_computation.1 | convolution fusion | flops 8388864 | bytes 917568 | tf_op jit(solution)/shard_map/kj,rjb->krb/dot_general | solution.py:418
  1.3 0.3 copy.6.grad_ref
  1.6 0.0 copy-start
  1.6 1.6 %copy-done = bf16[1024,1,1024]{2,0,1:T(8,128)(2,1)S(1)} copy-done((bf16[1024,1,1024]{2,0,1:T(8,128)(2,1)S(1)}, bf16[1024,1,1024]{2,0,1:T(8,128)(2,1)}, u32[]{:S(2)}) %copy-start) | copy-done | bytes 2097176
  3.2 2.7 %shard_map.37.part_ref = f32[4608,128]{1,0:T(8,128)S(1)} custom-call(bf16[1024,1024]{1,0:T(8,128)(2,1)S(1)} %bitcast.5), custom_call_target="tpu_custom_call" | custom-call | tf_op jit(solution)/shard_map/pallas_call | solution.py:251
  5.9 60.2 %shard_map.38 = (f32[4608,128]{1,0:T(8,128)S(1)}, bf16[16,16,1024]{2,1,0:T(8,128)(2,1)S(1)}) custom-call(f32[4608,128]{1,0:T(8,128)S(1)} %shard_map.37.part_ref, bf16[16,16,1024]{2,1,0:T(8,128)(2,1)S(1)} %copy.6.grad_ref), custom_call_target="tpu_custom_call" | custom-call | tf_op jit(solution)/shard_map/pallas_call | solution.py:234
  66.1 27.8 %shard_map.39 = bf16[192,1024]{1,0:T(8,128)(2,1)} custom-call(f32[4608,128]{1,0:T(8,128)S(1)} %get-tuple-element.7.s_ref, bf16[16,16,1024]{2,1,0:T(8,128)(2,1)S(1)} %get-tuple-element.8.g_ref), custom_call_target="tpu_custom_call" | custom-call | tf_op jit(solution)/shard_map/pallas_call | solution.py:405
Async XLA Ops:
  1.6 1.6 %copy-start = (bf16[1024,1,1024]{2,0,1:T(8,128)(2,1)S(1)}, bf16[1024,1,1024]{2,0,1:T(8,128)(2,1)}, u32[]{:S(2)}) copy-start(bf16[1024,1,1024]{2,0,1:T(8,128)(2,1)} %param.3) | copy-start | bytes 6291460

commit v6 on v5

--- a/solution.py
+++ b/solution.py
@@ -17,12 +17,14 @@
 
 
 def covariance_kernel(act_ref, out_ref):
-    for j in range(8):
-        column = act_ref[:, j * B : (j + 1) * B]
+    for j in range(0, 8, 2):
+        columns = act_ref[:, j * B : (j + 2) * B]
         part = lax.dot_general(
-            act_ref[:, j * B :], column, (((0,), (0,)), ((), ())), preferred_element_type=F32
+            act_ref[:, j * B :], columns, (((0,), (0,)), ((), ())), preferred_element_type=F32
         )
-        out_ref[pl.ds(block_rows(j, j), (8 - j) * B), :] = part
+        n = (8 - j) * B
+        out_ref[pl.ds(block_rows(j, j), n), :] = part[:, :B]
+        out_ref[pl.ds(block_rows(j + 1, j + 1), n - B), :] = part[B:, B:]
 
 
 def exchange_body(part_ref, grad_ref, sum_ref, tile_ref, acc, from_core, from_x, za_plus, za_minus, zb_plus, zb_minus, xa,

time: 94.1 us -> 93 us (0.988)
  Pallas kernels: 90.8 us -> 89.6 us
    pallas_call x1, Pallas kernels: 2.69 us -> 1.58 us  [covariance(): pl.pallas_call(covariance_kernel, out_shape=jax.ShapeDtypeStruct((4608, B...]
where the time goes in v6:
time: 93 us; the launch traced here: 92.8 us
  Pallas kernels  89.6 us (96%)
  local copies, waits for them, and re-layouts  1.88 us (2%)
  matrix products  1.27 us (1%)
    pallas_call x1, Pallas kernels, exchange(): pl.pallas_call(exchange_body, out_shape=(jax.ShapeDtypeStruct((4608, B),...  60.2 us
    pallas_call x1, Pallas kernels, factor(): pl.pallas_call(functools.partial(factor_kernel, tokens), out_shape=jax.Sh...  27.8 us

profile of v6, /device:TPU:1, one launch (start us, length us, event | category | flops | bytes accessed | tf_op | source)
XLA Modules:
  0.0 92.8 jit_solution(11677688417791896730)
XLA Ops:
  0.0 1.3 %fusion = bf16[16,16,1024]{2,0,1:T(8,128)(2,1)S(1)} fusion(bf16[12,16,1024]{2,1,0:T(8,128)(2,1)} %param.4, s32[16]{0:T(128)} %param.5), kind=kOutput, calls=%fused_computation.1 | convolution fusion | flops 8388864 | bytes 917568 | tf_op jit(solution)/shard_map/kj,rjb->krb/dot_general | solution.py:420
  1.3 0.3 copy.6.grad_ref
  1.6 0.0 copy-start
  1.6 1.6 %copy-done = bf16[1024,1,1024]{2,0,1:T(8,128)(2,1)S(1)} copy-done((bf16[1024,1,1024]{2,0,1:T(8,128)(2,1)S(1)}, bf16[1024,1,1024]{2,0,1:T(8,128)(2,1)}, u32[]{:S(2)}) %copy-start) | copy-done | bytes 2097176
  3.2 1.6 %shard_map.37.part_ref = f32[4608,128]{1,0:T(8,128)S(1)} custom-call(bf16[1024,1024]{1,0:T(8,128)(2,1)S(1)} %bitcast.5), custom_call_target="tpu_custom_call" | custom-call | tf_op jit(solution)/shard_map/pallas_call | solution.py:253
  4.8 60.2 %shard_map.38 = (f32[4608,128]{1,0:T(8,128)S(1)}, bf16[16,16,1024]{2,1,0:T(8,128)(2,1)S(1)}) custom-call(f32[4608,128]{1,0:T(8,128)S(1)} %shard_map.37.part_ref, bf16[16,16,1024]{2,1,0:T(8,128)(2,1)S(1)} %copy.6.grad_ref), custom_call_target="tpu_custom_call" | custom-call | tf_op jit(solution)/shard_map/pallas_call | solution.py:236
  65.0 27.8 %shard_map.39 = bf16[192,1024]{1,0:T(8,128)(2,1)} custom-call(f32[4608,128]{1,0:T(8,128)S(1)} %get-tuple-element.7.s_ref, bf16[16,16,1024]{2,1,0:T(8,128)(2,1)S(1)} %get-tuple-element.8.g_ref), custom_call_target="tpu_custom_call" | custom-call | tf_op jit(solution)/shard_map/pallas_call | solution.py:407
Async XLA Ops:
  1.6 1.6 %copy-start = (bf16[1024,1,1024]{2,0,1:T(8,128)(2,1)S(1)}, bf16[1024,1,1024]{2,0,1:T(8,128)(2,1)}, u32[]{:S(2)}) copy-start(bf16[1024,1,1024]{2,0,1:T(8,128)(2,1)} %param.3) | copy-start | bytes 6291460
